TPU v7x, 32 devices: a whole 2x2x4 slice. The times are simulated.
32 devices in a mesh: rows: 8 (over z, y), cols: 4 (over x, core).
Axes of the slice: x: 2, y: 2, z: 4, core: 2. Of those that a mesh axis runs over, the one named last changes fastest.
Arguments:
- tracks: float32 [1024, 2, 16384], P(('rows', 'cols')), may hold values from -200 to 200
- pixel_order: int32 [16384], P('rows'), may hold values from 0 to 16383, as said below
- pairing: int32 [2, 4], replicated, may hold values from 0 to 2
Outputs:
- rotated: float32 [16384, 2048], P('rows', 'cols')
Inputs may be any that keep to these rules, and one draw needn't show every extreme that they name: `pixel_order`: A permutation of 0 to 16383 that maps each aligned block of 2048 rows onto the same block of pixels.
All inputs are finite; a program needn't handle non-finite values.
Results may differ from a plain program's by a relative error of at most 0.0001.
Values sent between devices are 32-bit elements; how exact they have to be, the bound alone decides.
No kernel may reach another device: no remote copies, remote signals or barrier semaphores. Data moves between devices by JAX's collectives and lax.ppermute only.
A program may use at most 64 MiB of HBM per device.

v0:
```python
import jax
import jax.numpy as jnp
from jax import lax
from jax.experimental import pallas as pl
from jax.experimental.pallas import tpu as pltpu
from jax.sharding import PartitionSpec as P

STEPS = 2
NS_STEPS = 6
SLOTS = 4
LANES = 128
WAYS = 2
PARTS = 4
MIB = 1024 * 1024

F32 = jnp.float32
BF16 = jnp.bfloat16
NN = (((1,), (0,)), ((), ()))
NT = (((1,), (1,)), ((), ()))
TN = (((0,), (0,)), ((), ()))

ANY = pl.BlockSpec(memory_space=pl.ANY)
HBM = pl.BlockSpec(memory_space=pltpu.HBM)
SMEM = pl.BlockSpec(memory_space=pltpu.SMEM)
VMEM = pl.BlockSpec(memory_space=pltpu.VMEM)


def pair_slots(chosen):
    partner = 2 - chosen
    low = jnp.where(partner == 0, 1, 0)
    high = jnp.where(partner == 2, 1, 2)
    return partner, low, high


def params(mib, flops=0, moved=0):
    return dict(
        compiler_params=pltpu.CompilerParams(vmem_limit_bytes=mib * MIB),
        cost_estimate=pl.CostEstimate(flops=int(flops), bytes_accessed=int(moved), transcendentals=0),
    )


def like(*arrays):
    return [jax.ShapeDtypeStruct(a.shape, a.dtype) for a in arrays]


def halves(value):
    high = value.astype(BF16)
    return high, (value - high.astype(F32)).astype(BF16)


def thirds(value):
    high = value.astype(BF16)
    rest = value - high.astype(F32)
    middle = rest.astype(BF16)
    return high, middle, (rest - middle.astype(F32)).astype(BF16)


def mul(a, b, dims=NN):
    return lax.dot_general(a, b, dims, preferred_element_type=F32)


def mul_split(a, b, dims=NN):
    return mul(a[0], b[0], dims) + (mul(a[0], b[1], dims) + mul(a[1], b[0], dims))


def dot_split(a, b, dims=NN):
    return mul_split(halves(a), halves(b), dims)


def identity(size):
    return lax.broadcasted_iota(jnp.int32, (size, size), 0) == lax.broadcasted_iota(jnp.int32, (size, size), 1)


def span(index, width):
    return pl.ds(pl.multiple_of(index * width, width), width)


def spread_kernel(tracks_ref, pieces_ref, came_ref, ready_ref, in_sems, out_sems):
    row_devices, frames, _, rows = came_ref.shape
    loads = [
        pltpu.make_async_copy(tracks_ref.at[:, :, pl.ds(r * rows, rows)], came_ref.at[r], in_sems.at[r])
        for r in range(row_devices)
    ]
    stores = [
        pltpu.make_async_copy(ready_ref.at[r], pieces_ref.at[r], out_sems.at[r]) for r in range(row_devices)
    ]
    for load in loads:
        load.start()
    for r in range(row_devices):
        loads[r].wait()
        for component in range(2):
            plane = came_ref[r, :, component, :]
            for group in range(frames // 8):
                for half in range(2):
                    ready_ref[r, 2 * component + half, 4 * group:4 * group + 4, :] = plane[
                        8 * group + 4 * half:8 * group + 4 * half + 4, :]
        stores[r].start()
    for store in stores:
        store.wait()


def spread(tracks, row_devices):
    frames, _, pixels = tracks.shape
    rows = pixels // row_devices
    shape = (row_devices, 4, frames // 2, rows)
    return pl.pallas_call(
        spread_kernel,
        in_specs=[ANY],
        out_specs=HBM,
        out_shape=jax.ShapeDtypeStruct(shape, F32),
        scratch_shapes=[
            pltpu.VMEM((row_devices, frames, 2, rows), F32),
            pltpu.VMEM(shape, F32),
            pltpu.SemaphoreType.DMA((row_devices,)),
            pltpu.SemaphoreType.DMA((row_devices,)),
        ],
        name="spread",
        **params(61, 0, 8 * tracks.size),
    )(tracks)


def loads_of(held_ref, came_ref, sems):
    loads = [
        pltpu.make_async_copy(held_ref.at[:, pl.ds(k * LANES, LANES)], came_ref.at[k], sems.at[k])
        for k in range(came_ref.shape[0])
    ]
    for load in loads:
        load.start()
    return loads


def loads_scratch(columns, rows):
    return [pltpu.VMEM((rows // LANES, columns, LANES), F32), pltpu.SemaphoreType.DMA((rows // LANES,))]


def coupling_kernel(chosen_ref, held_ref, sums_ref, last_ref, came_ref, sems):
    tiles = came_ref.shape[0]
    width = sums_ref.shape[1]
    loads = loads_of(held_ref, came_ref, sems)
    partner, first, second = pair_slots(chosen_ref[0])
    products = [jnp.zeros((2 * width, 2 * width), F32)] * 2
    squares = [jnp.zeros((width, LANES), F32)] * SLOTS
    for part in range(0, tiles, WAYS):
        here = range(part, part + WAYS)
        for k in here:
            loads[k].wait()
        for index, slots in enumerate(((partner, SLOTS - 1), (first, second))):
            both = []
            for side, slot in enumerate(slots):
                pieces = [came_ref[k, pl.ds(slot, width, SLOTS), :] for k in here]
                for piece in pieces:
                    squares[2 * index + side] += piece * piece
                block = jnp.concatenate(pieces, axis=1)
                if index == 0:
                    last_ref[side * width:(side + 1) * width, part * LANES:(part + WAYS) * LANES] = block
                both.append(jnp.concatenate(halves(block), axis=0))
            products[index] += mul(both[0], both[1], NT)
    for index, product in enumerate(products):
        top = product[:width, :width] + (product[:width, width:] + product[width:, :width])
        sums_ref[index * width:(index + 1) * width, :] = top + product[width:, width:]
    rows = [jnp.sum(squared.T, axis=0, keepdims=True) for squared in squares]
    sums_ref[2 * width:, :] = jnp.concatenate(rows + [jnp.zeros((4, width), F32)], axis=0)


def couplings(chosen, held):
    columns, rows = held.shape
    width = columns // SLOTS
    return pl.pallas_call(
        coupling_kernel,
        in_specs=[SMEM, ANY],
        out_specs=[VMEM] * 2,
        out_shape=[
            jax.ShapeDtypeStruct((2 * width + 8, width), F32),
            jax.ShapeDtypeStruct((2 * width, rows), F32),
        ],
        scratch_shapes=loads_scratch(columns, rows),
        name="couplings",
        **params(16, 16 * width * width * rows, 6 * held.size),
    )(chosen, held)


def gram_kernel(value_ref, held_ref, carried_ref, gram_ref, split_ref, came_ref, sems):
    tiles = came_ref.shape[0]
    columns = gram_ref.shape[0]
    width = columns // SLOTS
    loads = loads_of(held_ref, came_ref, sems)
    carried_ref[...] = value_ref[...]
    cross = 0.0
    for half in range(2):
        here = range(half * tiles // 2, (half + 1) * tiles // 2)
        for k in here:
            loads[k].wait()
            for slot in range(SLOTS):
                high, low = halves(came_ref[k, pl.ds(slot, width, SLOTS), :])
                lanes = slice(k * LANES, (k + 1) * LANES)
                split_ref[slot * width:(slot + 1) * width, lanes] = high
                split_ref[columns + slot * width:columns + (slot + 1) * width, lanes] = low
        lanes = slice(here.start * LANES, here.stop * LANES)
        high = split_ref[:columns, lanes]
        cross += mul(high, split_ref[columns:, lanes], NT)
        if half == 0:
            gram_ref[...] = mul(high, high, NT)
        else:
            gram_ref[...] += mul(high, high, NT) + (cross + cross.T)


def local_gram(value, held):
    columns, rows = held.shape
    return pl.pallas_call(
        gram_kernel,
        in_specs=[VMEM, ANY],
        out_specs=[VMEM] * 3,
        out_shape=like(value) + [
            jax.ShapeDtypeStruct((columns, columns), F32),
            jax.ShapeDtypeStruct((2 * columns, rows), BF16),
        ],
        scratch_shapes=loads_scratch(columns, rows),
        name="gram",
        **params(16, 4 * columns * columns * rows, 8 * columns * rows),
    )(value, held)


def left_terms(value):
    high, middle, low = thirds(value)
    return jnp.concatenate([high, middle], axis=1), jnp.concatenate([low, high], axis=1)


def right_terms(value):
    high, middle, low = thirds(value)
    wide = jnp.concatenate([high, middle], axis=1)
    return jnp.concatenate([wide, wide], axis=0), jnp.concatenate([high, low], axis=0)


def terms_product(left, right):
    width = left[0].shape[0]
    wide = mul(left[0], right[0])
    return wide[:, :width] + (wide[:, width:] + mul(left[1], right[1]))


def rotations(grams):
    width = grams[0][0].shape[0]
    eye = identity(width).astype(F32)
    couplings, scales, squares, products = [], [], [], []
    for block, row_sums, column_sums in grams:
        coupling = block / (jnp.broadcast_to(row_sums, (width, width)).T + column_sums)
        total = 1.0 + jnp.sum(coupling * coupling)
        couplings.append(coupling)
        flipped = coupling.T
        for one, two in ((coupling, flipped), (flipped, coupling)):
            scales.append(1.0 / jnp.sqrt(total))
            squares.append((eye + terms_product(left_terms(one), right_terms(two))) / total)
    for count in range(NS_STEPS):
        factors = [1.5 * eye - 0.5 * square for square in squares]
        rights = [right_terms(factor) for factor in factors]
        if count == 0:
            products = [scale * factor for scale, factor in zip(scales, factors)]
        else:
            products = [terms_product(left_terms(product), right) for product, right in zip(products, rights)]
        if count + 1 < NS_STEPS:
            for _ in range(2):
                squares = [terms_product(left_terms(square), right) for square, right in zip(squares, rights)]
    results = []
    for index, coupling in enumerate(couplings):
        across = terms_product(left_terms(products[2 * index]), right_terms(coupling))
        results.append((products[2 * index], across, -across.T, products[2 * index + 1]))
    return results


def rotation_kernel(one_ref, two_ref, rotation_ref, sent_ref):
    width = one_ref.shape[1]
    total = one_ref[...] + two_ref[...]
    sums = total[2 * width:]
    grams = [(total[:width], sums[0:1], sums[1:2]), (total[width:2 * width], sums[2:3], sums[3:4])]
    for index, (top, right, bottom, end) in enumerate(rotations(grams)):
        rotation_ref[index, :width, :width] = top
        rotation_ref[index, :width, width:] = right
        rotation_ref[index, width:, :width] = bottom
        rotation_ref[index, width:, width:] = end
        if index == 0:
            sent_ref[:width, :] = right
            sent_ref[width:, :] = end


def two_rotations(one, two):
    width = one.shape[1]
    return pl.pallas_call(
        rotation_kernel,
        in_specs=[VMEM] * 2,
        out_specs=[VMEM] * 2,
        out_shape=[
            jax.ShapeDtypeStruct((2, 2 * width, 2 * width), F32),
            jax.ShapeDtypeStruct((2 * width, width), F32),
        ],
        name="rotations",
        **params(16, 300 * 4 * width**3, 16 * width * width),
    )(one, two)


def own_kernel(chosen_ref, gram_ref, split_ref, came_ref, rotation_ref, sums_ref, meets_ref, pair_ref):
    width = sums_ref.shape[1]
    columns = SLOTS * width
    partner, first, second = pair_slots(chosen_ref[0])
    meets, low, high = pair_slots(chosen_ref[1])

    def place(slot):
        in_last = slot == partner
        members = (jnp.where(in_last, partner, first), jnp.where(in_last, SLOTS - 1, second))
        side = jnp.where(jnp.logical_or(in_last, slot == first), 0, 1)
        return members, rotation_ref[jnp.where(in_last, 0, 1), :, span(side, width)]

    def between(rows, others):
        return jnp.concatenate(
            [jnp.concatenate([gram_ref[span(r, width), span(c, width)] for c in others], axis=1) for r in rows], axis=0)

    def squares(gram, turn):
        return jnp.sum(turn * dot_split(gram, turn), axis=0, keepdims=True)

    (meets_in, meets_turn), (low_in, low_turn), (high_in, high_turn) = place(meets), place(low), place(high)
    here = [
        jnp.concatenate([split_ref[span(m + start, width), :] for m in meets_in], axis=0) for start in (0, SLOTS)
    ]
    came = halves(came_ref[...])
    meets_ref[...] = dot_split(meets_turn, mul_split(here, came, NT), TN)
    twice = mul(came[0], came[1], NT)
    pair_ref[...] = mul(came[0], came[0], NT) + (twice + twice.T)
    sums_ref[:width, :] = jnp.zeros((width, width), F32)
    sums_ref[width:2 * width, :] = dot_split(low_turn, dot_split(between(low_in, high_in), high_turn), TN)
    rows = [
        squares(between(meets_in, meets_in), meets_turn),
        jnp.zeros((1, width), F32),
        squares(between(low_in, low_in), low_turn),
        squares(between(high_in, high_in), high_turn),
        jnp.zeros((4, width), F32),
    ]
    sums_ref[2 * width:, :] = jnp.concatenate(rows, axis=0)


def own_sums(chosen, gram, split, came, turns):
    pair, rows = came.shape
    width = pair // 2
    return pl.pallas_call(
        own_kernel,
        in_specs=[SMEM] + [VMEM] * 4,
        out_specs=[VMEM] * 3,
        out_shape=[
            jax.ShapeDtypeStruct((2 * width + 8, width), F32),
            jax.ShapeDtypeStruct((width, pair), F32),
            jax.ShapeDtypeStruct((pair, pair), F32),
        ],
        name="own_sums",
        **params(16, 10 * pair * pair * rows, 8 * came.size),
    )(chosen, gram, split, came, turns)


def second_kernel(own_ref, meets_ref, pair_ref, turn_ref, sums_ref):
    width = sums_ref.shape[1]
    turn = turn_ref[...]
    split = halves(turn)
    sums_ref[...] = own_ref[...]
    sums_ref[:width, :] = mul_split(halves(meets_ref[...]), split)
    sums_ref[2 * width + 1:2 * width + 2, :] = jnp.sum(
        turn * mul_split(halves(pair_ref[...]), split), axis=0, keepdims=True)


def second_sums(own, meets, pair, came_turn):
    return pl.pallas_call(
        second_kernel,
        in_specs=[VMEM] * 4,
        out_specs=VMEM,
        out_shape=like(own)[0],
        name="second_sums",
        **params(8, 4 * pair.size * own.shape[1], 8 * pair.size),
    )(own, meets, pair, came_turn)


def picks(order_ref, rows):
    order = order_ref[...]
    return jnp.where(lax.broadcasted_iota(jnp.int32, (rows, order.shape[1]), 0) == order, 1.0, 0.0).astype(BF16)


def order_kernel(order_ref, split_ref, value_ref, *refs):
    carried_ref, matrix_ref = refs[-2:]
    width = matrix_ref.shape[3]

    @pl.when(pl.program_id(0) == 0)
    def _():
        carried_ref[...] = value_ref[...]

    both = mul(split_ref[...], picks(order_ref, split_ref.shape[1]))
    for term in range(2):
        for block in range(SLOTS):
            start = (term * SLOTS + block) * width
            matrix_ref[term, block] = both[start:start + width].T.astype(BF16)


def ordered(order, split, value, tiles, into=None):
    columns, rows = split.shape[0] // 2, split.shape[1]
    width = columns // SLOTS
    chunk = 2 * width
    start, stop = tiles
    extra = () if into is None else (into,)
    return pl.pallas_call(
        order_kernel,
        grid=(stop - start,),
        in_specs=[
            pl.BlockSpec((1, chunk), lambda k: (0, k + start)),
            VMEM,
            VMEM,
        ] + [ANY] * len(extra),
        out_specs=[VMEM, pl.BlockSpec((2, SLOTS, chunk, width), lambda k: (0, 0, k + start, 0))],
        out_shape=like(value) + [jax.ShapeDtypeStruct((2, SLOTS, rows, width), BF16)],
        input_output_aliases={} if into is None else {3: 1},
        name="row_order",
        **params(16, 4 * columns * rows * chunk * (stop - start), 8 * columns * rows),
    )(order, split, value, *extra)


def turn_kernel(chosen_ref, matrix_ref, rotation_ref, value_ref, carried_ref, turned_ref):
    width = matrix_ref.shape[3]
    partner, first, second = pair_slots(chosen_ref[0])

    @pl.when(pl.program_id(0) == 0)
    def _():
        carried_ref[...] = value_ref[...]

    for index, (one, two) in enumerate(((partner, SLOTS - 1), (first, second))):
        pair = [jnp.concatenate([matrix_ref[term, one], matrix_ref[term, two]], axis=1) for term in range(2)]
        turned = mul_split(pair, halves(rotation_ref[index]))
        for term, part in enumerate(halves(turned)):
            turned_ref[term, one] = part[:, :width]
            turned_ref[term, two] = part[:, width:]


def turn(chosen, matrix, turns, value):
    _, _, rows, width = matrix.shape
    chunk = rows // 2
    blocks = pl.BlockSpec((2, SLOTS, chunk, width), lambda k: (0, 0, k, 0))
    return pl.pallas_call(
        turn_kernel,
        grid=(rows // chunk,),
        in_specs=[SMEM, blocks, VMEM, VMEM],
        out_specs=[VMEM, blocks],
        out_shape=like(value, matrix),
        name="first_turn",
        **params(20, 24 * rows * width * width, 4 * matrix.size),
    )(chosen, matrix, turns, value)


def take_kernel(chosen_ref, turned_ref, value_ref, carried_ref, block_ref):
    slot = 2 - chosen_ref[1]
    carried_ref[...] = value_ref[...]
    block_ref[...] = turned_ref[0, slot].astype(F32) + turned_ref[1, slot].astype(F32)


def taken(chosen, turned, value):
    _, _, rows, width = turned.shape
    return pl.pallas_call(
        take_kernel,
        in_specs=[SMEM, VMEM, VMEM],
        out_specs=[VMEM, VMEM],
        out_shape=like(value) + [jax.ShapeDtypeStruct((rows, width), F32)],
        name="taken",
        **params(8, 0, 8 * rows * width),
    )(chosen, turned, value)


def moved_kernel(order_ref, came_ref, turn_ref, value_ref, carried_ref, block_ref, split_ref):
    width = block_ref.shape[2]
    rows = came_ref.shape[1]

    @pl.when(pl.program_id(0) == 0)
    def _():
        carried_ref[...] = value_ref[...]
        high, low = halves(dot_split(turn_ref[...], came_ref[...], TN))
        split_ref[:width, :] = high
        split_ref[width:, :] = low

    both = mul(split_ref[...], picks(order_ref, rows))
    for term in range(2):
        block_ref[term] = both[term * width:(term + 1) * width].T.astype(BF16)


def moved_block(order, came, came_turn, value):
    pair, rows = came.shape
    width = pair // 2
    chunk = pair
    return pl.pallas_call(
        moved_kernel,
        grid=(rows // chunk,),
        in_specs=[
            pl.BlockSpec((1, chunk), lambda k: (0, k)),
            VMEM,
            VMEM,
            VMEM,
        ],
        out_specs=[VMEM, pl.BlockSpec((2, chunk, width), lambda k: (0, k, 0))],
        out_shape=like(value) + [jax.ShapeDtypeStruct((2, rows, width), BF16)],
        scratch_shapes=[pltpu.VMEM((pair, rows), BF16)],
        name="moved_block",
        **params(16, 4 * width * rows * rows, 8 * came.size),
    )(order, came, came_turn, value)


def most_kernel(chosen_ref, turned_ref, moved_ref, rotation_ref, out_ref, ready_ref, sems):
    rows, width = moved_ref.shape[1:]
    meets, low, high = pair_slots(chosen_ref[1])
    chunk = rows // PARTS
    pair_turn = halves(rotation_ref[1])
    meets_turn = halves(rotation_ref[0, :, :width])
    stores = []
    for part in range(PARTS):
        here = pl.ds(part * chunk, chunk)

        def beside(one, two):
            return [jnp.concatenate([one[term], two[term]], axis=1) for term in range(2)]

        def block(slot, here=here):
            return [turned_ref[term, slot, here] for term in range(2)]

        pair = mul_split(beside(block(low), block(high)), pair_turn)
        ready_ref[here, span(low, width)] = pair[:, :width]
        ready_ref[here, span(high, width)] = pair[:, width:]
        ready_ref[here, span(meets, width)] = mul_split(
            beside(block(meets), [moved_ref[term, here] for term in range(2)]), meets_turn)
        stores.append(pltpu.make_async_copy(
            ready_ref.at[here], out_ref.at[here, pl.ds(0, (SLOTS - 1) * width)], sems.at[part]))
        stores[-1].start()
    for store in stores:
        store.wait()


def most_slots(chosen, turned, moved, turns):
    _, _, rows, width = turned.shape
    return pl.pallas_call(
        most_kernel,
        in_specs=[SMEM] + [VMEM] * 3,
        out_specs=ANY,
        out_shape=jax.ShapeDtypeStruct((rows, SLOTS * width), F32),
        scratch_shapes=[pltpu.VMEM((rows, (SLOTS - 1) * width), F32), pltpu.SemaphoreType.DMA((PARTS,))],
        name="second_turn",
        **params(16, 18 * rows * width * width, 4 * turned.size),
    )(chosen, turned, moved, turns)


def rest_kernel(turned_ref, behind_ref, turn_ref, _, out_ref, ready_ref, sems):
    rows, width = behind_ref.shape
    chunk = rows // PARTS
    split = halves(turn_ref[...])
    stores = []
    for part in range(PARTS):
        here = pl.ds(part * chunk, chunk)
        pair = [
            jnp.concatenate([one, turned_ref[term, SLOTS - 1, here]], axis=1)
            for term, one in enumerate(halves(behind_ref[here]))
        ]
        ready_ref[here] = mul_split(pair, split)
        stores.append(pltpu.make_async_copy(
            ready_ref.at[here], out_ref.at[here, pl.ds((SLOTS - 1) * width, width)], sems.at[part]))
        stores[-1].start()
    for store in stores:
        store.wait()


def last_slot(turned, behind, behind_turn, out):
    _, _, rows, width = turned.shape
    return pl.pallas_call(
        rest_kernel,
        in_specs=[VMEM] * 3 + [ANY],
        out_specs=ANY,
        out_shape=like(out)[0],
        scratch_shapes=[pltpu.VMEM((rows, width), F32), pltpu.SemaphoreType.DMA((PARTS,))],
        input_output_aliases={3: 0},
        name="last_slot",
        **params(16, 12 * rows * width * width, 12 * rows * width),
    )(turned, behind, behind_turn, out)


def from_behind(value, axis, steps):
    count = lax.axis_size(axis)
    pairs = [(source, (source + steps) % count) for source in range(count)]
    return lax.ppermute(value, axis, pairs)


def summed(value, axis, beside):
    count = lax.axis_size(axis)
    got = jnp.zeros_like(value)
    if count & (count - 1):
        value, count = lax.psum(value, axis), 1
    distance = 1
    while distance < count:
        if distance > 1:
            value = value + got
        got = lax.ppermute(value, axis, [(source, source ^ distance) for source in range(count)])
        if beside:
            value = beside.pop(0)(value)
        distance *= 2
    for work in beside:
        value = work(value)
    return value, got


def body(tracks, pixel_order, pairing):
    frames_dev, _, pixel_total = tracks.shape
    row_devices = lax.axis_size("rows")
    row_count = pixel_total // row_devices
    pieces = spread(tracks, row_devices).reshape(row_devices * 4, frames_dev // 2, row_count)
    arrived = lax.all_to_all(pieces, ("rows", "cols"), split_axis=0, concat_axis=0, tiled=True)
    held = arrived.reshape(-1, row_count)
    order = (pixel_order - lax.axis_index("rows") * row_count).reshape(1, row_count)
    chosen = lax.dynamic_index_in_dim(pairing, lax.axis_index("cols"), axis=1, keepdims=False)
    tiles = row_count // (held.shape[0] // 2)
    kept = {}

    def gram_work(value):
        value, kept["gram"], kept["split"] = local_gram(value, held)
        return value

    def order_first(value):
        value, kept["matrix"] = ordered(order, kept["split"], value, (0, tiles // 2))
        return value

    def order_rest(value):
        value, kept["matrix"] = ordered(order, kept["split"], value, (tiles // 2, tiles), kept["matrix"])
        return value

    def turn_work(value):
        value, kept["turned"] = turn(chosen, kept["matrix"], turns, value)
        return value

    def taken_work(value):
        value, meets = taken(chosen, kept["turned"], value)
        kept["behind"] = from_behind(meets, "cols", -1)
        return value

    def moved_work(value):
        value, kept["moved"] = moved_block(order, came, came_turn, value)
        return value

    sums, last = couplings(chosen, held)
    came = from_behind(last, "cols", 1)
    turns, sent = two_rotations(*summed(sums, "rows", [gram_work, order_first, order_rest]))
    came_turn = from_behind(sent, "cols", 1)
    own, meets, pair = own_sums(chosen, kept["gram"], kept["split"], came, turns)
    sums = second_sums(own, meets, pair, came_turn)

    second_turns, sent = two_rotations(*summed(sums, "rows", [turn_work, taken_work, moved_work]))
    behind_turn = from_behind(sent, "cols", -1)
    out = most_slots(chosen, kept["turned"], kept["moved"], second_turns)
    return last_slot(kept["turned"], kept["behind"], behind_turn, out)


def solution(mesh):
    placed = (P(("rows", "cols"), None, None), P("rows"), P())
    return jax.shard_map(
        body, mesh=mesh, in_specs=placed, out_specs=P("rows", "cols"), check_vma=False
    )
```

profile of v0, /device:TPU:1, one launch (start us, length us, event | category | flops | bytes accessed | tf_op | source)
XLA Modules:
  0.0 170.6 jit_solution(7232983575526882515)
XLA Ops:
  0.0 0.0 copy-start
  0.0 3.5 %spread.1 = f32[8,4,16,2048]{3,2,1,0:T(8,128)} custom-call(f32[32,2,16384]{2,1,0:T(2,128)} %tracks_ref.1), custom_call_target="tpu_custom_call" | custom-call | bytes 8388608 | tf_op jit(solution)/shard_map/spread/pallas_call | solution.py:106
  3.5 7.2 %all-to-all-start = ((f32[32,16,2048]{2,1,0:T(8,128)}), f32[32,16,2048]{2,1,0:T(8,128)}, u32[]{:S(2)}, u32[]{:S(2)}) async-start(f32[32,16,2048]{2,1,0:T(8,128)} %bitcast.6), calls=%async_computation | async-start | bytes 8388608 | tf_op jit(solution)/shard_map/all_to_all | solution.py:607
  10.7 0.0 copy-start.1
  10.7 0.0 copy-done
  10.7 0.2 dynamic-slice_reduce_fusion.chosen_ref
  10.9 93.1 %all-to-all-done = f32[32,16,2048]{2,1,0:T(8,128)} async-done(((f32[32,16,2048]{2,1,0:T(8,128)}), f32[32,16,2048]{2,1,0:T(8,128)}, u32[]{:S(2)}, u32[]{:S(2)}) %all-to-all-start) | async-done | bytes 4194336 | tf_op jit(solution)/shard_map/all_to_all | solution.py:607
  104.0 4.4 %couplings.1 = (f32[264,128]{1,0:T(8,128)S(1)}, f32[256,2048]{1,0:T(8,128)}) custom-call(s32[2]{0:T(128)S(1)} %dynamic-slice_reduce_fusion.chosen_ref, f32[512,2048]{1,0:T(8,128)} %bitcast.2.held_ref), custom_call_target="tpu_custom_call" | custom-call | flops 536870912 | bytes 6291456 | tf_op jit(solution)/shard_map/couplings/pallas_call | solution.py:168
  108.4 1.8 %collective-permute-start.3 = (f32[256,2048]{1,0:T(8,128)}, f32[256,2048]{1,0:T(8,128)S(1)}, u32[]{:S(2)}, u32[]{:S(2)}) collective-permute-start(f32[256,2048]{1,0:T(8,128)} %get-tuple-element.36), channel_id=1, source_target_pairs={{0,1},{1,2},{2,3},{3,0},{4,5},{5,6},{6,7},{7,4},{8,9},{9,10},{10,1... | collective-permute-start | bytes 6291464 | tf_op jit(solution)/shard_map/ppermute | solution.py:581
  110.2 0.0 copy-done.1
  110.2 1.4 collective-permute-start
  111.7 4.8 %gram.1 = (f32[264,128]{1,0:T(8,128)S(1)}, f32[512,512]{1,0:T(8,128)S(1)}, bf16[1024,2048]{1,0:T(8,128)(2,1)S(1)}) custom-call(f32[264,128]{1,0:T(8,128)S(1)} %get-tuple-element.27.value_ref, f32[512,2048]{1,0:T(8,128)} %bitcast.2.held_ref), custom_call_target="tpu_custom_call" | custom-call | flops 2147483648 | bytes 8388608 | tf_op jit(solution)/shard_map/gram/pallas_call | solution.py:209
  116.5 0.0 collective-permute-done
  116.5 0.1 collective-permute-start.1
  116.6 5.4 %row_order.2 = (f32[264,128]{1,0:T(8,128)S(1)}, bf16[2,4,2048,128]{3,2,1,0:T(8,128)(2,1)S(1)}) custom-call(s32[1,2048]{1,0:T(1,128)S(1)} %bitcast.3, bf16[1024,2048]{1,0:T(8,128)(2,1)S(1)} %get-tuple-element.28.split_ref, f32[264,128]{1,0:T(8,128)S(1)} %add.17.value_ref), custom_call_target="tpu_custom_call" | custom-call | flops 4294967296 | bytes 8388608 | tf_op jit(solution)/shard_map/row_order/pallas_call | solution.py:402
  122.0 0.0 collective-permute-done.1
  122.1 1.8 %collective-permute-start.2 = (f32[264,128]{1,0:T(8,128)S(1)}, f32[264,128]{1,0:T(8,128)S(1)}, u32[]{:S(2)}, u32[]{:S(2)}) collective-permute-start(f32[264,128]{1,0:T(8,128)S(1)} %add.18.value_ref), channel_id=1, source_target_pairs={{0,16},{4,20},{8,24},{12,28},{16,0},{20,4},{24,8},{28,12},{1,17},{... | collective-permute-start | bytes 405512 | tf_op jit(solution)/shard_map/ppermute | solution.py:593
  123.9 5.4 %row_order.3 = (f32[264,128]{1,0:T(8,128)S(1)}, bf16[2,4,2048,128]{3,2,1,0:T(8,128)(2,1)S(1)}) custom-call(s32[1,2048]{1,0:T(1,128)S(1)} %bitcast.4, bf16[1024,2048]{1,0:T(8,128)(2,1)S(1)} %get-tuple-element.28.split_ref, f32[264,128]{1,0:T(8,128)S(1)} %add.18.value_ref, ...), custom_call_target="tpu_custom_call", output_to_operand_aliasing={{1}: (3, {})} | custom-call | flops 4294967296 | bytes 8388608 | tf_op jit(solution)/shard_map/row_order/pallas_call | solution.py:402
  129.3 2.1 %collective-permute-done.2.two_ref = f32[264,128]{1,0:T(8,128)S(1)} collective-permute-done((f32[264,128]{1,0:T(8,128)S(1)}, f32[264,128]{1,0:T(8,128)S(1)}, u32[]{:S(2)}, u32[]{:S(2)}) %collective-permute-start.2) | collective-permute-done | bytes 135200 | tf_op jit(solution)/shard_map/ppermute | solution.py:593
  131.4 3.0 %rotations.2 = (f32[2,256,256]{2,1,0:T(8,128)S(1)}, f32[256,128]{1,0:T(8,128)S(1)}) custom-call(f32[264,128]{1,0:T(8,128)S(1)} %get-tuple-element.33.one_ref, f32[264,128]{1,0:T(8,128)S(1)} %collective-permute-done.2.two_ref), custom_call_target="tpu_custom_call" | custom-call | flops 2516582400 | bytes 262144 | tf_op jit(solution)/shard_map/rotations/pallas_call | solution.py:286
  134.4 0.7 collective-permute-start.4
  135.1 0.0 collective-permute-done.3.came_ref
  135.1 4.5 %own_sums.1 = (f32[264,128]{1,0:T(8,128)S(1)}, f32[128,256]{1,0:T(8,128)S(1)}, f32[256,256]{1,0:T(8,128)S(1)}) custom-call(s32[2]{0:T(128)S(1)} %dynamic-slice_reduce_fusion.chosen_ref, f32[512,512]{1,0:T(8,128)S(1)} %get-tuple-element.35.gram_ref, bf16[1024,2048]{1,0:T(8,128)(2,1)S(1)} %get-tuple-element.28.split_ref, ...), custom_call_target="tpu_custom_call" | custom-call | flops 1342177280 | bytes 4194304 | tf_op jit(solution)/shard_map/own_sums/pallas_call | solution.py:341
  139.6 0.0 collective-permute-done.4.turn_ref
  139.7 0.3 second_sums.1.value_ref
  140.0 0.6 collective-permute-start.5
  140.6 3.3 %first_turn.1 = (f32[264,128]{1,0:T(8,128)S(1)}, bf16[2,4,2048,128]{3,2,1,0:T(8,128)(2,1)S(1)}) custom-call(s32[2]{0:T(128)S(1)} %dynamic-slice_reduce_fusion.chosen_ref, bf16[2,4,2048,128]{3,2,1,0:T(8,128)(2,1)S(1)} %get-tuple-element.32.matrix_ref, f32[2,256,256]{2,1,0:T(8,128)S(1)} %get-tuple-element.34.rotation_ref, f32[264,128]{1,0:T(8,128)S(1)} %second_sums.1.value_ref), custom_call_target="tpu_custom_call" | custom-call | flops 805306368 | bytes 8388608 | tf_op jit(solution)/shard_map/first_turn/pallas_call | solution.py:438
  143.8 1.2 collective-permute-done.5
  145.1 0.7 taken.1
  145.8 1.0 collective-permute-start.6
  146.8 0.0 collective-permute-start.7
  146.8 3.9 %collective-permute-done.7 = f32[264,128]{1,0:T(8,128)S(1)} collective-permute-done((f32[264,128]{1,0:T(8,128)S(1)}, f32[264,128]{1,0:T(8,128)S(1)}, u32[]{:S(2)}, u32[]{:S(2)}) %collective-permute-start.7) | collective-permute-done | bytes 135200 | tf_op jit(solution)/shard_map/ppermute | solution.py:593
  150.7 0.6 collective-permute-start.8
  151.3 5.0 %moved_block.1 = (f32[264,128]{1,0:T(8,128)S(1)}, bf16[2,2048,128]{2,1,0:T(8,128)(2,1)S(1)}) custom-call(s32[1,2048]{1,0:T(1,128)S(1)} %bitcast.5, f32[256,2048]{1,0:T(8,128)S(1)} %collective-permute-done.3.came_ref, f32[256,128]{1,0:T(8,128)S(1)} %collective-permute-done.4.turn_ref, f32[264,128]{1,0:T(8,128)S(1)} %add.20.value_ref), custom_call_target="tpu_custom_call" | custom-call | flops 2147483648 | bytes 4194304 | tf_op jit(solution)/shard_map/moved_block/pallas_call | solution.py:487
  156.3 2.2 %collective-permute-done.8.two_ref = f32[264,128]{1,0:T(8,128)S(1)} collective-permute-done((f32[264,128]{1,0:T(8,128)S(1)}, f32[264,128]{1,0:T(8,128)S(1)}, u32[]{:S(2)}, u32[]{:S(2)}) %collective-permute-start.8) | collective-permute-done | bytes 135200 | tf_op jit(solution)/shard_map/ppermute | solution.py:593
  158.5 3.0 %rotations.3 = (f32[2,256,256]{2,1,0:T(8,128)S(1)}, f32[256,128]{1,0:T(8,128)S(1)}) custom-call(f32[264,128]{1,0:T(8,128)S(1)} %get-tuple-element.45.one_ref, f32[264,128]{1,0:T(8,128)S(1)} %collective-permute-done.8.two_ref), custom_call_target="tpu_custom_call" | custom-call | flops 2516582400 | bytes 262144 | tf_op jit(solution)/shard_map/rotations/pallas_call | solution.py:286
  161.6 1.8 %collective-permute-start.9 = (f32[256,128]{1,0:T(8,128)S(1)}, f32[256,128]{1,0:T(8,128)S(1)}, u32[]{:S(2)}, u32[]{:S(2)}) collective-permute-start(f32[256,128]{1,0:T(8,128)S(1)} %get-tuple-element.46), channel_id=1, source_target_pairs={{0,3},{1,0},{2,1},{3,2},{4,7},{5,4},{6,5},{7,6},{8,11},{9,8},{10,9... | collective-permute-start | bytes 393224 | tf_op jit(solution)/shard_map/ppermute | solution.py:581
  163.4 3.3 %second_turn.1._ = f32[2048,512]{1,0:T(8,128)} custom-call(s32[2]{0:T(128)S(1)} %dynamic-slice_reduce_fusion.chosen_ref, bf16[2,4,2048,128]{3,2,1,0:T(8,128)(2,1)S(1)} %get-tuple-element.41.turned_ref, bf16[2,2048,128]{2,1,0:T(8,128)(2,1)S(1)} %get-tuple-element.47.moved_ref, f32[2,256,256]{2,1,0:T(8,128)S(1)} %get-tuple-element.48.rotation_ref), custom_call_target="tpu_custom_call" | custom-call | flops 603979776 | bytes 8388608 | tf_op jit(solution)/shard_map/second_turn/pallas_call | solution.py:534
  166.6 2.0 %collective-permute-done.9.turn_ref = f32[256,128]{1,0:T(8,128)S(1)} collective-permute-done((f32[256,128]{1,0:T(8,128)S(1)}, f32[256,128]{1,0:T(8,128)S(1)}, u32[]{:S(2)}, u32[]{:S(2)}) %collective-permute-start.9) | collective-permute-done | bytes 131104 | tf_op jit(solution)/shard_map/ppermute | solution.py:581
  168.6 0.0 collective-permute-done.6.behind_ref
  168.6 1.8 %last_slot.1 = f32[2048,512]{1,0:T(8,128)} custom-call(bf16[2,4,2048,128]{3,2,1,0:T(8,128)(2,1)S(1)} %get-tuple-element.41.turned_ref, f32[2048,128]{1,0:T(8,128)S(1)} %collective-permute-done.6.behind_ref, f32[256,128]{1,0:T(8,128)S(1)} %collective-permute-done.9.turn_ref, f32[2048,512]{1,0:T(8,128)} %second_turn.1._), custom_call_target="tpu_custom_call", output_to_operand_aliasing={{}: (3, {})} | custom-call | flops 402653184 | bytes 3145728 | tf_op jit(solution)/shard_map/last_slot/pallas_call | solution.py:566
  (5 shorter events, 0.1 us)
Async XLA Ops:
  0.0 10.7 %copy-start = (s32[2,4]{1,0:T(2,128)S(1)}, s32[2,4]{1,0:T(2,128)}, u32[]{:S(2)}) copy-start(s32[2,4]{1,0:T(2,128)} %param.5) | copy-start | bytes 100
  3.5 100.5 %all-to-all-start = ((f32[32,16,2048]{2,1,0:T(8,128)}), f32[32,16,2048]{2,1,0:T(8,128)}, u32[]{:S(2)}, u32[]{:S(2)}) async-start(f32[32,16,2048]{2,1,0:T(8,128)} %bitcast.6), calls=%async_computation | async-start | bytes 8388608 | tf_op jit(solution)/shard_map/all_to_all | solution.py:607
  10.7 99.6 %copy-start.1 = (s32[2048]{0:T(1024)S(1)}, s32[2048]{0:T(1024)}, u32[]{:S(2)}) copy-start(s32[2048]{0:T(1024)} %param.4) | copy-start | bytes 24580
  108.4 26.7 %collective-permute-start.3 = (f32[256,2048]{1,0:T(8,128)}, f32[256,2048]{1,0:T(8,128)S(1)}, u32[]{:S(2)}, u32[]{:S(2)}) collective-permute-start(f32[256,2048]{1,0:T(8,128)} %get-tuple-element.36), channel_id=1, source_target_pairs={{0,1},{1,2},{2,3},{3,0},{4,5},{5,6},{6,7},{7,4},{8,9},{9,10},{10,1... | collective-permute-start | bytes 6291464 | tf_op jit(solution)/shard_map/ppermute | solution.py:581
  110.2 6.3 %collective-permute-start = (f32[264,128]{1,0:T(8,128)S(1)}, f32[264,128]{1,0:T(8,128)S(1)}, u32[]{:S(2)}, u32[]{:S(2)}) collective-permute-start(f32[264,128]{1,0:T(8,128)S(1)} %get-tuple-element.27.value_ref), channel_id=1, source_target_pairs={{0,4},{4,0},{8,12},{12,8},{16,20},{20,16},{24,28},{28,24},{1,5},{5... | collective-permute-start | bytes 405512 | tf_op jit(solution)/shard_map/ppermute | solution.py:593
  116.5 5.5 %collective-permute-start.1 = (f32[264,128]{1,0:T(8,128)S(1)}, f32[264,128]{1,0:T(8,128)S(1)}, u32[]{:S(2)}, u32[]{:S(2)}) collective-permute-start(f32[264,128]{1,0:T(8,128)S(1)} %add.17.value_ref), channel_id=1, source_target_pairs={{0,8},{4,12},{8,0},{12,4},{16,24},{20,28},{24,16},{28,20},{1,9},{5... | collective-permute-start | bytes 405512 | tf_op jit(solution)/shard_map/ppermute | solution.py:593
  122.1 9.3 %collective-permute-start.2 = (f32[264,128]{1,0:T(8,128)S(1)}, f32[264,128]{1,0:T(8,128)S(1)}, u32[]{:S(2)}, u32[]{:S(2)}) collective-permute-start(f32[264,128]{1,0:T(8,128)S(1)} %add.18.value_ref), channel_id=1, source_target_pairs={{0,16},{4,20},{8,24},{12,28},{16,0},{20,4},{24,8},{28,12},{1,17},{... | collective-permute-start | bytes 405512 | tf_op jit(solution)/shard_map/ppermute | solution.py:593
  134.4 5.2 %collective-permute-start.4 = (f32[256,128]{1,0:T(8,128)S(1)}, f32[256,128]{1,0:T(8,128)S(1)}, u32[]{:S(2)}, u32[]{:S(2)}) collective-permute-start(f32[256,128]{1,0:T(8,128)S(1)} %get-tuple-element.40), channel_id=1, source_target_pairs={{0,1},{1,2},{2,3},{3,0},{4,5},{5,6},{6,7},{7,4},{8,9},{9,10},{10,1... | collective-permute-start | bytes 393224 | tf_op jit(solution)/shard_map/ppermute | solution.py:581
  140.0 5.1 %collective-permute-start.5 = (f32[264,128]{1,0:T(8,128)S(1)}, f32[264,128]{1,0:T(8,128)S(1)}, u32[]{:S(2)}, u32[]{:S(2)}) collective-permute-start(f32[264,128]{1,0:T(8,128)S(1)} %second_sums.1.value_ref), channel_id=1, source_target_pairs={{0,4},{4,0},{8,12},{12,8},{16,20},{20,16},{24,28},{28,24},{1,5},{5... | collective-permute-start | bytes 405512 | tf_op jit(solution)/shard_map/ppermute | solution.py:593
  145.8 22.8 %collective-permute-start.6 = (f32[2048,128]{1,0:T(8,128)S(1)}, f32[2048,128]{1,0:T(8,128)S(1)}, u32[]{:S(2)}, u32[]{:S(2)}) collective-permute-start(f32[2048,128]{1,0:T(8,128)S(1)} %get-tuple-element.43), channel_id=1, source_target_pairs={{0,3},{1,0},{2,1},{3,2},{4,7},{5,4},{6,5},{7,6},{8,11},{9,8},{10,9... | collective-permute-start | bytes 3145736 | tf_op jit(solution)/shard_map/ppermute | solution.py:581
  146.8 3.9 %collective-permute-start.7 = (f32[264,128]{1,0:T(8,128)S(1)}, f32[264,128]{1,0:T(8,128)S(1)}, u32[]{:S(2)}, u32[]{:S(2)}) collective-permute-start(f32[264,128]{1,0:T(8,128)S(1)} %add.19.value_ref), channel_id=1, source_target_pairs={{0,8},{4,12},{8,0},{12,4},{16,24},{20,28},{24,16},{28,20},{1,9},{5... | collective-permute-start | bytes 405512 | tf_op jit(solution)/shard_map/ppermute | solution.py:593
  150.7 7.9 %collective-permute-start.8 = (f32[264,128]{1,0:T(8,128)S(1)}, f32[264,128]{1,0:T(8,128)S(1)}, u32[]{:S(2)}, u32[]{:S(2)}) collective-permute-start(f32[264,128]{1,0:T(8,128)S(1)} %add.20.value_ref), channel_id=1, source_target_pairs={{0,16},{4,20},{8,24},{12,28},{16,0},{20,4},{24,8},{28,12},{1,17},{... | collective-permute-start | bytes 405512 | tf_op jit(solution)/shard_map/ppermute | solution.py:593
  161.6 7.0 %collective-permute-start.9 = (f32[256,128]{1,0:T(8,128)S(1)}, f32[256,128]{1,0:T(8,128)S(1)}, u32[]{:S(2)}, u32[]{:S(2)}) collective-permute-start(f32[256,128]{1,0:T(8,128)S(1)} %get-tuple-element.46), channel_id=1, source_target_pairs={{0,3},{1,0},{2,1},{3,2},{4,7},{5,4},{6,5},{7,6},{8,11},{9,8},{10,9... | collective-permute-start | bytes 393224 | tf_op jit(solution)/shard_map/ppermute | solution.py:581
where the time goes:
time: 171 us
  waiting for transfers between devices  105 us (61%)
  Pallas kernels  48.6 us (28%)
  starting transfers between devices  16.9 us (10%)
    all_to_all x1, waiting for transfers between devices, body(): lax.all_to_all(pieces, ('rows', 'cols'), split_axis=0, concat_axis=0, til...  93.1 us
    pallas_call x2, Pallas kernels, ordered(): pl.pallas_call(order_kernel, grid=(stop - start,), in_specs=[pl.BlockSpec...  10.8 us
    ppermute x6, waiting for transfers between devices, summed(): lax.ppermute(value, axis, [(source, source ^ distance) for source in rang...  9.42 us
    all_to_all x1, starting transfers between devices, body(): lax.all_to_all(pieces, ('rows', 'cols'), split_axis=0, concat_axis=0, til...  7.16 us
    pallas_call x2, Pallas kernels, two_rotations(): pl.pallas_call(rotation_kernel, in_specs=[VMEM] * 2, out_specs=[VMEM] * 2...  6.09 us
    ppermute x4, starting transfers between devices, from_behind(): return lax.ppermute(value, axis, pairs)  5.27 us
    pallas_call x1, Pallas kernels, moved_block(): pl.pallas_call(moved_kernel, grid=(rows // chunk,), in_specs=[pl.BlockSpe...  5.04 us
    pallas_call x1, Pallas kernels, local_gram(): pl.pallas_call(gram_kernel, in_specs=[VMEM, ANY], out_specs=[VMEM] * 3, o...  4.82 us
  transfers between devices with their start and end apart: 11, of which 6 were waited for; matrix products, arithmetic and copies ran while one was open for 0% of the time, Pallas kernels for 22%

commit v1 on v0

--- a/solution.py
+++ b/solution.py
@@ -10,7 +10,7 @@
 SLOTS = 4
 LANES = 128
 WAYS = 2
-PARTS = 4
+PARTS = 8
 MIB = 1024 * 1024
 
 F32 = jnp.float32
@@ -119,24 +119,15 @@
     )(tracks)
 
 
-def loads_of(held_ref, came_ref, sems):
+def coupling_kernel(chosen_ref, held_ref, sums_ref, one_ref, two_ref, came_ref, sems):
+    tiles = came_ref.shape[0]
+    width = sums_ref.shape[1]
     loads = [
         pltpu.make_async_copy(held_ref.at[:, pl.ds(k * LANES, LANES)], came_ref.at[k], sems.at[k])
-        for k in range(came_ref.shape[0])
+        for k in range(tiles)
     ]
     for load in loads:
         load.start()
-    return loads
-
-
-def loads_scratch(columns, rows):
-    return [pltpu.VMEM((rows // LANES, columns, LANES), F32), pltpu.SemaphoreType.DMA((rows // LANES,))]
-
-
-def coupling_kernel(chosen_ref, held_ref, sums_ref, last_ref, came_ref, sems):
-    tiles = came_ref.shape[0]
-    width = sums_ref.shape[1]
-    loads = loads_of(held_ref, came_ref, sems)
     partner, first, second = pair_slots(chosen_ref[0])
     products = [jnp.zeros((2 * width, 2 * width), F32)] * 2
     squares = [jnp.zeros((width, LANES), F32)] * SLOTS
@@ -152,7 +143,7 @@
                     squares[2 * index + side] += piece * piece
                 block = jnp.concatenate(pieces, axis=1)
                 if index == 0:
-                    last_ref[side * width:(side + 1) * width, part * LANES:(part + WAYS) * LANES] = block
+                    (one_ref, two_ref)[side][:, part * LANES:(part + WAYS) * LANES] = block
                 both.append(jnp.concatenate(halves(block), axis=0))
             products[index] += mul(both[0], both[1], NT)
     for index, product in enumerate(products):
@@ -168,28 +159,28 @@
     return pl.pallas_call(
         coupling_kernel,
         in_specs=[SMEM, ANY],
-        out_specs=[VMEM] * 2,
+        out_specs=[VMEM] * 4,
         out_shape=[
             jax.ShapeDtypeStruct((2 * width + 8, width), F32),
-            jax.ShapeDtypeStruct((2 * width, rows), F32),
+            jax.ShapeDtypeStruct((width, rows), F32),
+            jax.ShapeDtypeStruct((width, rows), F32),
+            jax.ShapeDtypeStruct((rows // LANES, columns, LANES), F32),
         ],
-        scratch_shapes=loads_scratch(columns, rows),
+        scratch_shapes=[pltpu.SemaphoreType.DMA((rows // LANES,))],
         name="couplings",
         **params(16, 16 * width * width * rows, 6 * held.size),
     )(chosen, held)
 
 
-def gram_kernel(value_ref, held_ref, carried_ref, gram_ref, split_ref, came_ref, sems):
+def gram_kernel(value_ref, came_ref, carried_ref, gram_ref, split_ref):
     tiles = came_ref.shape[0]
     columns = gram_ref.shape[0]
     width = columns // SLOTS
-    loads = loads_of(held_ref, came_ref, sems)
     carried_ref[...] = value_ref[...]
     cross = 0.0
     for half in range(2):
         here = range(half * tiles // 2, (half + 1) * tiles // 2)
         for k in here:
-            loads[k].wait()
             for slot in range(SLOTS):
                 high, low = halves(came_ref[k, pl.ds(slot, width, SLOTS), :])
                 lanes = slice(k * LANES, (k + 1) * LANES)
@@ -204,20 +195,20 @@
             gram_ref[...] += mul(high, high, NT) + (cross + cross.T)
 
 
-def local_gram(value, held):
-    columns, rows = held.shape
+def local_gram(value, came):
+    tiles, columns, lanes = came.shape
+    rows = tiles * lanes
     return pl.pallas_call(
         gram_kernel,
-        in_specs=[VMEM, ANY],
+        in_specs=[VMEM] * 2,
         out_specs=[VMEM] * 3,
         out_shape=like(value) + [
             jax.ShapeDtypeStruct((columns, columns), F32),
             jax.ShapeDtypeStruct((2 * columns, rows), BF16),
         ],
-        scratch_shapes=loads_scratch(columns, rows),
         name="gram",
         **params(16, 4 * columns * columns * rows, 8 * columns * rows),
-    )(value, held)
+    )(value, came)
 
 
 def left_terms(value):
@@ -232,7 +223,7 @@
 
 
 def terms_product(left, right):
-    width = left[0].shape[0]
+    width = right[1].shape[1]
     wide = mul(left[0], right[0])
     return wide[:, :width] + (wide[:, width:] + mul(left[1], right[1]))
 
@@ -240,7 +231,7 @@
 def rotations(grams):
     width = grams[0][0].shape[0]
     eye = identity(width).astype(F32)
-    couplings, scales, squares, products = [], [], [], []
+    couplings, scales, squares, products, crossed = [], [], [], [], []
     for block, row_sums, column_sums in grams:
         coupling = block / (jnp.broadcast_to(row_sums, (width, width)).T + column_sums)
         total = 1.0 + jnp.sum(coupling * coupling)
@@ -248,20 +239,31 @@
         flipped = coupling.T
         for one, two in ((coupling, flipped), (flipped, coupling)):
             scales.append(1.0 / jnp.sqrt(total))
-            squares.append((eye + terms_product(left_terms(one), right_terms(two))) / total)
+            squares.append((eye + terms_product(left_terms(one), right_terms(two))) * (1.0 / total))
     for count in range(NS_STEPS):
         factors = [1.5 * eye - 0.5 * square for square in squares]
         rights = [right_terms(factor) for factor in factors]
+        if count + 1 == NS_STEPS:
+            crossed = [
+                terms_product(left_terms(product), right_terms(coupling))
+                for product, coupling in zip(products[::2], couplings)
+            ]
+        last = count + 1 == NS_STEPS
         if count == 0:
             products = [scale * factor for scale, factor in zip(scales, factors)]
+        elif last:
+            products = [terms_product(left_terms(product), right) for product, right in zip(products, rights)]
         else:
-            products = [terms_product(left_terms(product), right) for product, right in zip(products, rights)]
-        if count + 1 < NS_STEPS:
-            for _ in range(2):
-                squares = [terms_product(left_terms(square), right) for square, right in zip(squares, rights)]
+            both = [jnp.concatenate([square, product], axis=0) for square, product in zip(squares, products)]
+            both = [terms_product(left_terms(one), right) for one, right in zip(both, rights)]
+            squares, products = [one[:width] for one in both], [one[width:] for one in both]
+        if count == 0:
+            squares = [terms_product(left_terms(square), right) for square, right in zip(squares, rights)]
+        if not last:
+            squares = [terms_product(left_terms(square), right) for square, right in zip(squares, rights)]
     results = []
-    for index, coupling in enumerate(couplings):
-        across = terms_product(left_terms(products[2 * index]), right_terms(coupling))
+    for index, half in enumerate(crossed):
+        across = terms_product(left_terms(factors[2 * index]), right_terms(half))
         results.append((products[2 * index], across, -across.T, products[2 * index + 1]))
     return results
 
@@ -296,17 +298,25 @@
     )(one, two)
 
 
-def own_kernel(chosen_ref, gram_ref, split_ref, came_ref, rotation_ref, sums_ref, meets_ref, pair_ref):
-    width = sums_ref.shape[1]
-    columns = SLOTS * width
+def near(split_ref, slots, width):
+    return [
+        jnp.concatenate([split_ref[span(slot + start, width), :] for slot in slots], axis=0) for start in (0, SLOTS)
+    ]
+
+
+def places(chosen_ref):
     partner, first, second = pair_slots(chosen_ref[0])
-    meets, low, high = pair_slots(chosen_ref[1])
 
     def place(slot):
         in_last = slot == partner
         members = (jnp.where(in_last, partner, first), jnp.where(in_last, SLOTS - 1, second))
-        side = jnp.where(jnp.logical_or(in_last, slot == first), 0, 1)
-        return members, rotation_ref[jnp.where(in_last, 0, 1), :, span(side, width)]
+        return members, jnp.where(in_last, 0, 1), jnp.where(jnp.logical_or(in_last, slot == first), 0, 1)
+
+    return [place(slot) for slot in pair_slots(chosen_ref[1])]
+
+
+def own_kernel(chosen_ref, gram_ref, split_ref, came_ref, rotation_ref, sums_ref, cross_ref, pair_ref):
+    width = sums_ref.shape[1]
 
     def between(rows, others):
         return jnp.concatenate(
@@ -315,14 +325,17 @@
     def squares(gram, turn):
         return jnp.sum(turn * dot_split(gram, turn), axis=0, keepdims=True)
 
-    (meets_in, meets_turn), (low_in, low_turn), (high_in, high_turn) = place(meets), place(low), place(high)
-    here = [
-        jnp.concatenate([split_ref[span(m + start, width), :] for m in meets_in], axis=0) for start in (0, SLOTS)
+    found = places(chosen_ref)
+    (meets_in, low_in, high_in), (meets_turn, low_turn, high_turn) = [members for members, _, _ in found], [
+        rotation_ref[pair, :, span(side, width)] for _, pair, side in found
     ]
+    here = near(split_ref, meets_in, width)
     came = halves(came_ref[...])
-    meets_ref[...] = dot_split(meets_turn, mul_split(here, came, NT), TN)
-    twice = mul(came[0], came[1], NT)
-    pair_ref[...] = mul(came[0], came[0], NT) + (twice + twice.T)
+    pair = 2 * width
+    by_high = mul(jnp.concatenate([*here, came[0]], axis=0), came[0], NT)
+    by_low = mul(jnp.concatenate([here[0], came[0]], axis=0), came[1], NT)
+    cross_ref[...] = by_high[:pair] + (by_high[pair:2 * pair] + by_low[:pair])
+    pair_ref[...] = by_high[2 * pair:] + (by_low[pair:] + by_low[pair:].T)
     sums_ref[:width, :] = jnp.zeros((width, width), F32)
     sums_ref[width:2 * width, :] = dot_split(low_turn, dot_split(between(low_in, high_in), high_turn), TN)
     rows = [
@@ -336,20 +349,54 @@
 
 
 def own_sums(chosen, gram, split, came, turns):
-    pair, rows = came.shape
-    width = pair // 2
+    width, rows = came.shape
     return pl.pallas_call(
         own_kernel,
         in_specs=[SMEM] + [VMEM] * 4,
         out_specs=[VMEM] * 3,
         out_shape=[
             jax.ShapeDtypeStruct((2 * width + 8, width), F32),
-            jax.ShapeDtypeStruct((width, pair), F32),
-            jax.ShapeDtypeStruct((pair, pair), F32),
+            jax.ShapeDtypeStruct((2 * width, width), F32),
+            jax.ShapeDtypeStruct((width, width), F32),
         ],
         name="own_sums",
-        **params(16, 10 * pair * pair * rows, 8 * came.size),
+        **params(16, 16 * width * width * rows, 24 * width * rows),
     )(chosen, gram, split, came, turns)
+
+
+def cross_kernel(chosen_ref, split_ref, first_ref, second_ref, cross_ref, top_ref, rotation_ref, meets_ref, pair_ref):
+    width = first_ref.shape[0]
+    members, index, side = places(chosen_ref)[0]
+    turn = rotation_ref[index, :, span(side, width)]
+    here = near(split_ref, members, width)
+    first, second = halves(first_ref[...]), halves(second_ref[...])
+    pair = 2 * width
+    by_high = mul(jnp.concatenate([*here, *first, second[0]], axis=0), second[0], NT)
+    by_low = mul(jnp.concatenate([here[0], first[0], second[0]], axis=0), second[1], NT)
+    cross = by_high[:pair] + (by_high[pair:2 * pair] + by_low[:pair])
+    meets_ref[...] = dot_split(turn, jnp.concatenate([cross_ref[...], cross], axis=1), TN)
+    rest = by_high[2 * pair:]
+    mixed = rest[:width] + (rest[width:pair] + by_low[pair:pair + width])
+    twice = by_low[pair + width:]
+    pair_ref[:width, :width] = top_ref[...]
+    pair_ref[:width, width:] = mixed
+    pair_ref[width:, :width] = mixed.T
+    pair_ref[width:, width:] = rest[pair:] + (twice + twice.T)
+
+
+def came_sums(chosen, split, came, cross, top, turns):
+    width, rows = came[0].shape
+    return pl.pallas_call(
+        cross_kernel,
+        in_specs=[SMEM] + [VMEM] * 6,
+        out_specs=[VMEM] * 2,
+        out_shape=[
+            jax.ShapeDtypeStruct((width, 2 * width), F32),
+            jax.ShapeDtypeStruct((2 * width, 2 * width), F32),
+        ],
+        name="came_sums",
+        **params(16, 16 * width * width * rows, 28 * width * rows),
+    )(chosen, split, *came, cross, top, turns)
 
 
 def second_kernel(own_ref, meets_ref, pair_ref, turn_ref, sums_ref):
@@ -415,7 +462,7 @@
     )(order, split, value, *extra)
 
 
-def turn_kernel(chosen_ref, matrix_ref, rotation_ref, value_ref, carried_ref, turned_ref):
+def turn_kernel(chosen_ref, matrix_ref, rotation_ref, value_ref, carried_ref, turned_ref, meets_ref):
     width = matrix_ref.shape[3]
     partner, first, second = pair_slots(chosen_ref[0])
 
@@ -429,6 +476,8 @@
         for term, part in enumerate(halves(turned)):
             turned_ref[term, one] = part[:, :width]
             turned_ref[term, two] = part[:, width:]
+    slot = 2 - chosen_ref[1]
+    meets_ref[...] = turned_ref[0, slot].astype(F32) + turned_ref[1, slot].astype(F32)
 
 
 def turn(chosen, matrix, turns, value):
@@ -439,39 +488,22 @@
         turn_kernel,
         grid=(rows // chunk,),
         in_specs=[SMEM, blocks, VMEM, VMEM],
-        out_specs=[VMEM, blocks],
-        out_shape=like(value, matrix),
+        out_specs=[VMEM, blocks, pl.BlockSpec((chunk, width), lambda k: (k, 0))],
+        out_shape=like(value, matrix) + [jax.ShapeDtypeStruct((rows, width), F32)],
         name="first_turn",
         **params(20, 24 * rows * width * width, 4 * matrix.size),
     )(chosen, matrix, turns, value)
 
 
-def take_kernel(chosen_ref, turned_ref, value_ref, carried_ref, block_ref):
-    slot = 2 - chosen_ref[1]
-    carried_ref[...] = value_ref[...]
-    block_ref[...] = turned_ref[0, slot].astype(F32) + turned_ref[1, slot].astype(F32)
-
-
-def taken(chosen, turned, value):
-    _, _, rows, width = turned.shape
-    return pl.pallas_call(
-        take_kernel,
-        in_specs=[SMEM, VMEM, VMEM],
-        out_specs=[VMEM, VMEM],
-        out_shape=like(value) + [jax.ShapeDtypeStruct((rows, width), F32)],
-        name="taken",
-        **params(8, 0, 8 * rows * width),
-    )(chosen, turned, value)
-
-
-def moved_kernel(order_ref, came_ref, turn_ref, value_ref, carried_ref, block_ref, split_ref):
+def moved_kernel(order_ref, one_ref, two_ref, turn_ref, value_ref, carried_ref, block_ref, split_ref):
     width = block_ref.shape[2]
-    rows = came_ref.shape[1]
+    rows = one_ref.shape[1]
 
     @pl.when(pl.program_id(0) == 0)
     def _():
         carried_ref[...] = value_ref[...]
-        high, low = halves(dot_split(turn_ref[...], came_ref[...], TN))
+        high, low = halves(
+            dot_split(turn_ref[...], jnp.concatenate([one_ref[...], two_ref[...]], axis=0), TN))
         split_ref[:width, :] = high
         split_ref[width:, :] = low
 
@@ -481,14 +513,14 @@
 
 
 def moved_block(order, came, came_turn, value):
-    pair, rows = came.shape
-    width = pair // 2
-    chunk = pair
+    width, rows = came[0].shape
+    pair = chunk = 2 * width
     return pl.pallas_call(
         moved_kernel,
         grid=(rows // chunk,),
         in_specs=[
             pl.BlockSpec((1, chunk), lambda k: (0, k)),
+            VMEM,
             VMEM,
             VMEM,
             VMEM,
@@ -497,8 +529,8 @@
         out_shape=like(value) + [jax.ShapeDtypeStruct((2, rows, width), BF16)],
         scratch_shapes=[pltpu.VMEM((pair, rows), BF16)],
         name="moved_block",
-        **params(16, 4 * width * rows * rows, 8 * came.size),
-    )(order, came, came_turn, value)
+        **params(16, 4 * width * rows * rows, 8 * pair * rows),
+    )(order, *came, came_turn, value)
 
 
 def most_kernel(chosen_ref, turned_ref, moved_ref, rotation_ref, out_ref, ready_ref, sems):
@@ -608,27 +640,27 @@
     held = arrived.reshape(-1, row_count)
     order = (pixel_order - lax.axis_index("rows") * row_count).reshape(1, row_count)
     chosen = lax.dynamic_index_in_dim(pairing, lax.axis_index("cols"), axis=1, keepdims=False)
-    tiles = row_count // (held.shape[0] // 2)
+    chunks = row_count // (held.shape[0] // 2)
     kept = {}
 
     def gram_work(value):
-        value, kept["gram"], kept["split"] = local_gram(value, held)
+        value, kept["gram"], kept["split"] = local_gram(value, tiles)
         return value
 
     def order_first(value):
-        value, kept["matrix"] = ordered(order, kept["split"], value, (0, tiles // 2))
+        value, kept["matrix"] = ordered(order, kept["split"], value, (0, chunks * 3 // 8))
         return value
 
     def order_rest(value):
-        value, kept["matrix"] = ordered(order, kept["split"], value, (tiles // 2, tiles), kept["matrix"])
+        value, kept["matrix"] = ordered(order, kept["split"], value, (chunks * 3 // 8, chunks), kept["matrix"])
         return value
 
     def turn_work(value):
-        value, kept["turned"] = turn(chosen, kept["matrix"], turns, value)
+        value, kept["turned"], kept["meets"] = turn(chosen, kept["matrix"], turns, value)
         return value
 
     def taken_work(value):
-        value, meets = taken(chosen, kept["turned"], value)
+        value, meets = lax.optimization_barrier((value, kept["meets"]))
         kept["behind"] = from_behind(meets, "cols", -1)
         return value
 
@@ -636,11 +668,12 @@
         value, kept["moved"] = moved_block(order, came, came_turn, value)
         return value
 
-    sums, last = couplings(chosen, held)
-    came = from_behind(last, "cols", 1)
+    sums, *last, tiles = couplings(chosen, held)
+    came = [from_behind(block, "cols", 1) for block in last]
     turns, sent = two_rotations(*summed(sums, "rows", [gram_work, order_first, order_rest]))
     came_turn = from_behind(sent, "cols", 1)
-    own, meets, pair = own_sums(chosen, kept["gram"], kept["split"], came, turns)
+    own, cross, top = own_sums(chosen, kept["gram"], kept["split"], came[0], turns)
+    meets, pair = came_sums(chosen, kept["split"], came, cross, top, turns)
     sums = second_sums(own, meets, pair, came_turn)
 
     second_turns, sent = two_rotations(*summed(sums, "rows", [turn_work, taken_work, moved_work]))

time: 171 us -> 167 us (0.977)
  Pallas kernels: 48.6 us -> 44.8 us
  waiting for transfers between devices: 105 us -> 103 us
    pallas_call x1, Pallas kernels: 4.54 us -> 2.4 us  [own_sums(): pl.pallas_call(own_kernel, in_specs=[SMEM] + [VMEM] * 4, out_specs=[VMEM]...]
    ppermute x4 -> x5, starting transfers between devices: 5.27 us -> 6.56 us  [from_behind(): return lax.ppermute(value, axis, pairs)]
  transfers between devices with their start and end apart: 11 -> 12, of which waited for: 6 -> 7; matrix products, arithmetic and copies ran while one was open for 0% -> 0% of each run, Pallas kernels for 22% -> 22%
where the time goes in v1:
time: 167 us
  waiting for transfers between devices  103 us (62%)
  Pallas kernels  44.8 us (27%)
  starting transfers between devices  17.9 us (11%)
    all_to_all x1, waiting for transfers between devices, body(): lax.all_to_all(pieces, ('rows', 'cols'), split_axis=0, concat_axis=0, til...  93.1 us
    pallas_call x2, Pallas kernels, ordered(): pl.pallas_call(order_kernel, grid=(stop - start,), in_specs=[pl.BlockSpec...  10.8 us
    ppermute x6, waiting for transfers between devices, summed(): lax.ppermute(value, axis, [(source, source ^ distance) for source in rang...  8.51 us
    all_to_all x1, starting transfers between devices, body(): lax.all_to_all(pieces, ('rows', 'cols'), split_axis=0, concat_axis=0, til...  7.16 us
    ppermute x5, starting transfers between devices, from_behind(): return lax.ppermute(value, axis, pairs)  6.56 us
    pallas_call x2, Pallas kernels, two_rotations(): pl.pallas_call(rotation_kernel, in_specs=[VMEM] * 2, out_specs=[VMEM] * 2...  6.1 us
    pallas_call x1, Pallas kernels, moved_block(): pl.pallas_call(moved_kernel, grid=(rows // chunk,), in_specs=[pl.BlockSpe...  5.01 us
    ppermute x6, starting transfers between devices, summed(): lax.ppermute(value, axis, [(source, source ^ distance) for source in rang...  4.18 us
  transfers between devices with their start and end apart: 12, of which 7 were waited for; matrix products, arithmetic and copies ran while one was open for 0% of the time, Pallas kernels for 22%

profile of v1, /device:TPU:1, one launch (start us, length us, event | category | flops | bytes accessed | tf_op | source)
XLA Modules:
  0.0 166.7 jit_solution(3378051029159709518)
XLA Ops:
  0.0 0.0 copy-start
  0.0 3.5 %spread.1 = f32[8,4,16,2048]{3,2,1,0:T(8,128)} custom-call(f32[32,2,16384]{2,1,0:T(2,128)} %tracks_ref.1), custom_call_target="tpu_custom_call" | custom-call | bytes 8388608 | tf_op jit(solution)/shard_map/spread/pallas_call | solution.py:106
  3.5 0.0 copy-start.1
  3.5 7.2 %all-to-all-start = ((f32[32,16,2048]{2,1,0:T(8,128)}), f32[32,16,2048]{2,1,0:T(8,128)}, u32[]{:S(2)}, u32[]{:S(2)}) async-start(f32[32,16,2048]{2,1,0:T(8,128)} %bitcast.6), calls=%async_computation | async-start | bytes 8388608 | tf_op jit(solution)/shard_map/all_to_all | solution.py:639
  10.7 0.0 copy-done
  10.7 0.2 dynamic-slice_reduce_fusion.chosen_ref
  10.9 0.0 copy-done.1
  10.9 93.1 %all-to-all-done = f32[32,16,2048]{2,1,0:T(8,128)} async-done(((f32[32,16,2048]{2,1,0:T(8,128)}), f32[32,16,2048]{2,1,0:T(8,128)}, u32[]{:S(2)}, u32[]{:S(2)}) %all-to-all-start) | async-done | bytes 4194336 | tf_op jit(solution)/shard_map/all_to_all | solution.py:639
  104.0 3.4 %couplings.1 = (f32[264,128]{1,0:T(8,128)S(1)}, f32[128,2048]{1,0:T(8,128)S(1)}, f32[128,2048]{1,0:T(8,128)S(1)}, f32[16,512,128]{2,1,0:T(8,128)S(1)}) custom-call(s32[2]{0:T(128)S(1)} %dynamic-slice_reduce_fusion.chosen_ref, f32[512,2048]{1,0:T(8,128)} %bitcast.2.held_ref), custom_call_target="tpu_custom_call" | custom-call | flops 536870912 | bytes 6291456 | tf_op jit(solution)/shard_map/couplings/pallas_call | solution.py:159
  107.4 1.0 collective-permute-start
  108.4 2.5 %collective-permute-start.3 = (f32[128,2048]{1,0:T(8,128)S(1)}, f32[128,2048]{1,0:T(8,128)S(1)}, u32[]{:S(2)}, u32[]{:S(2)}) collective-permute-start(f32[128,2048]{1,0:T(8,128)S(1)} %get-tuple-element.42), channel_id=1, source_target_pairs={{0,1},{1,2},{2,3},{3,0},{4,5},{5,6},{6,7},{7,4},{8,9},{9,10},{10,1... | collective-permute-start | bytes 3145736 | tf_op jit(solution)/shard_map/ppermute | solution.py:613
  110.9 0.0 collective-permute-start.4
  110.9 2.6 %gram.1 = (f32[264,128]{1,0:T(8,128)S(1)}, f32[512,512]{1,0:T(8,128)S(1)}, bf16[1024,2048]{1,0:T(8,128)(2,1)S(1)}) custom-call(f32[264,128]{1,0:T(8,128)S(1)} %get-tuple-element.32.value_ref, f32[16,512,128]{2,1,0:T(8,128)S(1)} %get-tuple-element.33.came_ref), custom_call_target="tpu_custom_call" | custom-call | flops 2147483648 | bytes 8388608 | tf_op jit(solution)/shard_map/gram/pallas_call | solution.py:201
  113.5 0.0 collective-permute-done
  113.5 0.1 collective-permute-start.1
  113.6 4.1 %row_order.2 = (f32[264,128]{1,0:T(8,128)S(1)}, bf16[2,4,2048,128]{3,2,1,0:T(8,128)(2,1)S(1)}) custom-call(s32[1,2048]{1,0:T(1,128)S(1)} %bitcast.3, bf16[1024,2048]{1,0:T(8,128)(2,1)S(1)} %get-tuple-element.34.split_ref, f32[264,128]{1,0:T(8,128)S(1)} %add.17.value_ref), custom_call_target="tpu_custom_call" | custom-call | flops 3221225472 | bytes 8388608 | tf_op jit(solution)/shard_map/row_order/pallas_call | solution.py:449
  117.7 0.6 collective-permute-done.1
  118.3 1.2 collective-permute-start.2
  119.5 6.8 %row_order.3 = (f32[264,128]{1,0:T(8,128)S(1)}, bf16[2,4,2048,128]{3,2,1,0:T(8,128)(2,1)S(1)}) custom-call(s32[1,2048]{1,0:T(1,128)S(1)} %bitcast.4, bf16[1024,2048]{1,0:T(8,128)(2,1)S(1)} %get-tuple-element.34.split_ref, f32[264,128]{1,0:T(8,128)S(1)} %add.18.value_ref, ...), custom_call_target="tpu_custom_call", output_to_operand_aliasing={{1}: (3, {})} | custom-call | flops 5368709120 | bytes 8388608 | tf_op jit(solution)/shard_map/row_order/pallas_call | solution.py:449
  126.3 0.7 collective-permute-done.2.two_ref
  127.0 3.1 %rotations.2 = (f32[2,256,256]{2,1,0:T(8,128)S(1)}, f32[256,128]{1,0:T(8,128)S(1)}) custom-call(f32[264,128]{1,0:T(8,128)S(1)} %get-tuple-element.39.one_ref, f32[264,128]{1,0:T(8,128)S(1)} %collective-permute-done.2.two_ref), custom_call_target="tpu_custom_call" | custom-call | flops 2516582400 | bytes 262144 | tf_op jit(solution)/shard_map/rotations/pallas_call | solution.py:288
  130.1 1.2 collective-permute-start.5
  131.3 0.0 collective-permute-done.3.came_ref.first_ref.one_ref
  131.3 2.4 %own_sums.1 = (f32[264,128]{1,0:T(8,128)S(1)}, f32[256,128]{1,0:T(8,128)S(1)}, f32[128,128]{1,0:T(8,128)S(1)}) custom-call(s32[2]{0:T(128)S(1)} %dynamic-slice_reduce_fusion.chosen_ref, f32[512,512]{1,0:T(8,128)S(1)} %get-tuple-element.41.gram_ref, bf16[1024,2048]{1,0:T(8,128)(2,1)S(1)} %get-tuple-element.34.split_ref, ...), custom_call_target="tpu_custom_call" | custom-call | flops 536870912 | bytes 6291456 | tf_op jit(solution)/shard_map/own_sums/pallas_call | solution.py:353
  133.7 0.1 collective-permute-done.4.second_ref.two_ref
  133.9 2.4 %came_sums.1 = (f32[128,256]{1,0:T(8,128)S(1)}, f32[256,256]{1,0:T(8,128)S(1)}) custom-call(s32[2]{0:T(128)S(1)} %dynamic-slice_reduce_fusion.chosen_ref, bf16[1024,2048]{1,0:T(8,128)(2,1)S(1)} %get-tuple-element.34.split_ref, f32[128,2048]{1,0:T(8,128)S(1)} %collective-permute-done.3.came_ref.first_ref.one_ref, ...), custom_call_target="tpu_custom_call" | custom-call | flops 536870912 | bytes 7340032 | tf_op jit(solution)/shard_map/came_sums/pallas_call | solution.py:389
  136.3 0.0 collective-permute-done.5.turn_ref
  136.3 0.3 second_sums.1.value_ref
  136.6 1.4 collective-permute-start.6
  138.0 3.4 %first_turn.1 = (f32[264,128]{1,0:T(8,128)S(1)}, bf16[2,4,2048,128]{3,2,1,0:T(8,128)(2,1)S(1)}, f32[2048,128]{1,0:T(8,128)S(1)}) custom-call(s32[2]{0:T(128)S(1)} %dynamic-slice_reduce_fusion.chosen_ref, bf16[2,4,2048,128]{3,2,1,0:T(8,128)(2,1)S(1)} %get-tuple-element.38.matrix_ref, f32[2,256,256]{2,1,0:T(8,128)S(1)} %get-tuple-element.40.rotation_ref, ...), custom_call_target="tpu_custom_call" | custom-call | flops 805306368 | bytes 8388608 | tf_op jit(solution)/shard_map/first_turn/pallas_call | solution.py:487
  141.4 0.0 collective-permute-done.6
  141.5 1.4 collective-permute-start.7
  142.9 0.4 collective-permute-start.8
  143.3 4.8 %collective-permute-done.8 = f32[264,128]{1,0:T(8,128)S(1)} collective-permute-done((f32[264,128]{1,0:T(8,128)S(1)}, f32[264,128]{1,0:T(8,128)S(1)}, u32[]{:S(2)}, u32[]{:S(2)}) %collective-permute-start.8) | collective-permute-done | bytes 135200 | tf_op jit(solution)/shard_map/ppermute | solution.py:625
  148.1 0.1 collective-permute-start.9
  148.2 5.0 %moved_block.1 = (f32[264,128]{1,0:T(8,128)S(1)}, bf16[2,2048,128]{2,1,0:T(8,128)(2,1)S(1)}) custom-call(s32[1,2048]{1,0:T(1,128)S(1)} %bitcast.5, f32[128,2048]{1,0:T(8,128)S(1)} %collective-permute-done.3.came_ref.first_ref.one_ref, f32[128,2048]{1,0:T(8,128)S(1)} %collective-permute-done.4.second_ref.two_ref, ...), custom_call_target="tpu_custom_call" | custom-call | flops 2147483648 | bytes 4194304 | tf_op jit(solution)/shard_map/moved_block/pallas_call | solution.py:518
  153.2 2.4 %collective-permute-done.9.two_ref = f32[264,128]{1,0:T(8,128)S(1)} collective-permute-done((f32[264,128]{1,0:T(8,128)S(1)}, f32[264,128]{1,0:T(8,128)S(1)}, u32[]{:S(2)}, u32[]{:S(2)}) %collective-permute-start.9) | collective-permute-done | bytes 135200 | tf_op jit(solution)/shard_map/ppermute | solution.py:625
  155.6 3.0 %rotations.3 = (f32[2,256,256]{2,1,0:T(8,128)S(1)}, f32[256,128]{1,0:T(8,128)S(1)}) custom-call(f32[264,128]{1,0:T(8,128)S(1)} %get-tuple-element.55.one_ref, f32[264,128]{1,0:T(8,128)S(1)} %collective-permute-done.9.two_ref), custom_call_target="tpu_custom_call" | custom-call | flops 2516582400 | bytes 262144 | tf_op jit(solution)/shard_map/rotations/pallas_call | solution.py:288
  158.7 1.4 collective-permute-start.10
  160.0 3.1 %second_turn.1._ = f32[2048,512]{1,0:T(8,128)} custom-call(s32[2]{0:T(128)S(1)} %dynamic-slice_reduce_fusion.chosen_ref, bf16[2,4,2048,128]{3,2,1,0:T(8,128)(2,1)S(1)} %get-tuple-element.50.turned_ref, bf16[2,2048,128]{2,1,0:T(8,128)(2,1)S(1)} %get-tuple-element.57.moved_ref, f32[2,256,256]{2,1,0:T(8,128)S(1)} %get-tuple-element.58.rotation_ref), custom_call_target="tpu_custom_call" | custom-call | flops 603979776 | bytes 8388608 | tf_op jit(solution)/shard_map/second_turn/pallas_call | solution.py:566
  163.2 1.7 %collective-permute-done.10.turn_ref = f32[256,128]{1,0:T(8,128)S(1)} collective-permute-done((f32[256,128]{1,0:T(8,128)S(1)}, f32[256,128]{1,0:T(8,128)S(1)}, u32[]{:S(2)}, u32[]{:S(2)}) %collective-permute-start.10) | collective-permute-done | bytes 131104 | tf_op jit(solution)/shard_map/ppermute | solution.py:613
  164.9 0.0 collective-permute-done.7.behind_ref
  164.9 1.7 %last_slot.1 = f32[2048,512]{1,0:T(8,128)} custom-call(bf16[2,4,2048,128]{3,2,1,0:T(8,128)(2,1)S(1)} %get-tuple-element.50.turned_ref, f32[2048,128]{1,0:T(8,128)S(1)} %collective-permute-done.7.behind_ref, f32[256,128]{1,0:T(8,128)S(1)} %collective-permute-done.10.turn_ref, f32[2048,512]{1,0:T(8,128)} %second_turn.1._), custom_call_target="tpu_custom_call", output_to_operand_aliasing={{}: (3, {})} | custom-call | flops 402653184 | bytes 3145728 | tf_op jit(solution)/shard_map/last_slot/pallas_call | solution.py:598
  (5 shorter events, 0.1 us)
Async XLA Ops:
  0.0 10.7 %copy-start = (s32[2,4]{1,0:T(2,128)S(1)}, s32[2,4]{1,0:T(2,128)}, u32[]{:S(2)}) copy-start(s32[2,4]{1,0:T(2,128)} %param.5) | copy-start | bytes 100
  3.5 7.4 %copy-start.1 = (s32[2048]{0:T(1024)S(1)}, s32[2048]{0:T(1024)}, u32[]{:S(2)}) copy-start(s32[2048]{0:T(1024)} %param.4) | copy-start | bytes 24580
  3.5 100.5 %all-to-all-start = ((f32[32,16,2048]{2,1,0:T(8,128)}), f32[32,16,2048]{2,1,0:T(8,128)}, u32[]{:S(2)}, u32[]{:S(2)}) async-start(f32[32,16,2048]{2,1,0:T(8,128)} %bitcast.6), calls=%async_computation | async-start | bytes 8388608 | tf_op jit(solution)/shard_map/all_to_all | solution.py:639
  107.4 6.1 %collective-permute-start = (f32[264,128]{1,0:T(8,128)S(1)}, f32[264,128]{1,0:T(8,128)S(1)}, u32[]{:S(2)}, u32[]{:S(2)}) collective-permute-start(f32[264,128]{1,0:T(8,128)S(1)} %get-tuple-element.32.value_ref), channel_id=1, source_target_pairs={{0,4},{4,0},{8,12},{12,8},{16,20},{20,16},{24,28},{28,24},{1,5},{5... | collective-permute-start | bytes 405512 | tf_op jit(solution)/shard_map/ppermute | solution.py:625
  108.4 22.9 %collective-permute-start.3 = (f32[128,2048]{1,0:T(8,128)S(1)}, f32[128,2048]{1,0:T(8,128)S(1)}, u32[]{:S(2)}, u32[]{:S(2)}) collective-permute-start(f32[128,2048]{1,0:T(8,128)S(1)} %get-tuple-element.42), channel_id=1, source_target_pairs={{0,1},{1,2},{2,3},{3,0},{4,5},{5,6},{6,7},{7,4},{8,9},{9,10},{10,1... | collective-permute-start | bytes 3145736 | tf_op jit(solution)/shard_map/ppermute | solution.py:613
  110.9 23.0 %collective-permute-start.4 = (f32[128,2048]{1,0:T(8,128)S(1)}, f32[128,2048]{1,0:T(8,128)S(1)}, u32[]{:S(2)}, u32[]{:S(2)}) collective-permute-start(f32[128,2048]{1,0:T(8,128)S(1)} %get-tuple-element.44), channel_id=1, source_target_pairs={{0,1},{1,2},{2,3},{3,0},{4,5},{5,6},{6,7},{7,4},{8,9},{9,10},{10,1... | collective-permute-start | bytes 3145736 | tf_op jit(solution)/shard_map/ppermute | solution.py:613
  113.5 4.7 %collective-permute-start.1 = (f32[264,128]{1,0:T(8,128)S(1)}, f32[264,128]{1,0:T(8,128)S(1)}, u32[]{:S(2)}, u32[]{:S(2)}) collective-permute-start(f32[264,128]{1,0:T(8,128)S(1)} %add.17.value_ref), channel_id=1, source_target_pairs={{0,8},{4,12},{8,0},{12,4},{16,24},{20,28},{24,16},{28,20},{1,9},{5... | collective-permute-start | bytes 405512 | tf_op jit(solution)/shard_map/ppermute | solution.py:625
  118.3 8.7 %collective-permute-start.2 = (f32[264,128]{1,0:T(8,128)S(1)}, f32[264,128]{1,0:T(8,128)S(1)}, u32[]{:S(2)}, u32[]{:S(2)}) collective-permute-start(f32[264,128]{1,0:T(8,128)S(1)} %add.18.value_ref), channel_id=1, source_target_pairs={{0,16},{4,20},{8,24},{12,28},{16,0},{20,4},{24,8},{28,12},{1,17},{... | collective-permute-start | bytes 405512 | tf_op jit(solution)/shard_map/ppermute | solution.py:625
  130.1 6.2 %collective-permute-start.5 = (f32[256,128]{1,0:T(8,128)S(1)}, f32[256,128]{1,0:T(8,128)S(1)}, u32[]{:S(2)}, u32[]{:S(2)}) collective-permute-start(f32[256,128]{1,0:T(8,128)S(1)} %get-tuple-element.49), channel_id=1, source_target_pairs={{0,1},{1,2},{2,3},{3,0},{4,5},{5,6},{6,7},{7,4},{8,9},{9,10},{10,1... | collective-permute-start | bytes 393224 | tf_op jit(solution)/shard_map/ppermute | solution.py:613
  136.6 4.8 %collective-permute-start.6 = (f32[264,128]{1,0:T(8,128)S(1)}, f32[264,128]{1,0:T(8,128)S(1)}, u32[]{:S(2)}, u32[]{:S(2)}) collective-permute-start(f32[264,128]{1,0:T(8,128)S(1)} %second_sums.1.value_ref), channel_id=1, source_target_pairs={{0,4},{4,0},{8,12},{12,8},{16,20},{20,16},{24,28},{28,24},{1,5},{5... | collective-permute-start | bytes 405512 | tf_op jit(solution)/shard_map/ppermute | solution.py:625
  141.5 23.4 %collective-permute-start.7 = (f32[2048,128]{1,0:T(8,128)S(1)}, f32[2048,128]{1,0:T(8,128)S(1)}, u32[]{:S(2)}, u32[]{:S(2)}) collective-permute-start(f32[2048,128]{1,0:T(8,128)S(1)} %get-tuple-element.53), channel_id=1, source_target_pairs={{0,3},{1,0},{2,1},{3,2},{4,7},{5,4},{6,5},{7,6},{8,11},{9,8},{10,9... | collective-permute-start | bytes 3145736 | tf_op jit(solution)/shard_map/ppermute | solution.py:613
  142.9 5.2 %collective-permute-start.8 = (f32[264,128]{1,0:T(8,128)S(1)}, f32[264,128]{1,0:T(8,128)S(1)}, u32[]{:S(2)}, u32[]{:S(2)}) collective-permute-start(f32[264,128]{1,0:T(8,128)S(1)} %add.19), channel_id=1, source_target_pairs={{0,8},{4,12},{8,0},{12,4},{16,24},{20,28},{24,16},{28,20},{1,9},{5... | collective-permute-start | bytes 405512 | tf_op jit(solution)/shard_map/ppermute | solution.py:625
  148.1 7.5 %collective-permute-start.9 = (f32[264,128]{1,0:T(8,128)S(1)}, f32[264,128]{1,0:T(8,128)S(1)}, u32[]{:S(2)}, u32[]{:S(2)}) collective-permute-start(f32[264,128]{1,0:T(8,128)S(1)} %add.20.value_ref), channel_id=1, source_target_pairs={{0,16},{4,20},{8,24},{12,28},{16,0},{20,4},{24,8},{28,12},{1,17},{... | collective-permute-start | bytes 405512 | tf_op jit(solution)/shard_map/ppermute | solution.py:625
  158.7 6.2 %collective-permute-start.10 = (f32[256,128]{1,0:T(8,128)S(1)}, f32[256,128]{1,0:T(8,128)S(1)}, u32[]{:S(2)}, u32[]{:S(2)}) collective-permute-start(f32[256,128]{1,0:T(8,128)S(1)} %get-tuple-element.56), channel_id=1, source_target_pairs={{0,3},{1,0},{2,1},{3,2},{4,7},{5,4},{6,5},{7,6},{8,11},{9,8},{10,9... | collective-permute-start | bytes 393224 | tf_op jit(solution)/shard_map/ppermute | solution.py:613

commit v2 on v1

--- a/solution.py
+++ b/solution.py
@@ -1,3 +1,5 @@
+import functools
+
 import jax
 import jax.numpy as jnp
 from jax import lax
@@ -143,7 +145,9 @@
                     squares[2 * index + side] += piece * piece
                 block = jnp.concatenate(pieces, axis=1)
                 if index == 0:
-                    (one_ref, two_ref)[side][:, part * LANES:(part + WAYS) * LANES] = block
+                    half, place = divmod(part, tiles // 2)
+                    (one_ref, two_ref)[half][
+                        side * width:(side + 1) * width, place * LANES:(place + WAYS) * LANES] = block
                 both.append(jnp.concatenate(halves(block), axis=0))
             products[index] += mul(both[0], both[1], NT)
     for index, product in enumerate(products):
@@ -162,8 +166,8 @@
         out_specs=[VMEM] * 4,
         out_shape=[
             jax.ShapeDtypeStruct((2 * width + 8, width), F32),
-            jax.ShapeDtypeStruct((width, rows), F32),
-            jax.ShapeDtypeStruct((width, rows), F32),
+            jax.ShapeDtypeStruct((2 * width, rows // 2), F32),
+            jax.ShapeDtypeStruct((2 * width, rows // 2), F32),
             jax.ShapeDtypeStruct((rows // LANES, columns, LANES), F32),
         ],
         scratch_shapes=[pltpu.SemaphoreType.DMA((rows // LANES,))],
@@ -268,11 +272,8 @@
     return results
 
 
-def rotation_kernel(one_ref, two_ref, rotation_ref, sent_ref):
-    width = one_ref.shape[1]
-    total = one_ref[...] + two_ref[...]
-    sums = total[2 * width:]
-    grams = [(total[:width], sums[0:1], sums[1:2]), (total[width:2 * width], sums[2:3], sums[3:4])]
+def put_rotations(grams, rotation_ref, sent_ref):
+    width = sent_ref.shape[1]
     for index, (top, right, bottom, end) in enumerate(rotations(grams)):
         rotation_ref[index, :width, :width] = top
         rotation_ref[index, :width, width:] = right
@@ -281,6 +282,14 @@
         if index == 0:
             sent_ref[:width, :] = right
             sent_ref[width:, :] = end
+
+
+def rotation_kernel(one_ref, two_ref, rotation_ref, sent_ref):
+    width = one_ref.shape[1]
+    total = one_ref[...] + two_ref[...]
+    sums = total[2 * width:]
+    put_rotations(
+        [(total[:width], sums[0:1], sums[1:2]), (total[width:2 * width], sums[2:3], sums[3:4])], rotation_ref, sent_ref)
 
 
 def two_rotations(one, two):
@@ -298,239 +307,213 @@
     )(one, two)
 
 
-def near(split_ref, slots, width):
-    return [
-        jnp.concatenate([split_ref[span(slot + start, width), :] for slot in slots], axis=0) for start in (0, SLOTS)
-    ]
-
-
-def places(chosen_ref):
+def places(chosen_ref, rotation_ref):
+    width = rotation_ref.shape[1] // 2
     partner, first, second = pair_slots(chosen_ref[0])
 
     def place(slot):
         in_last = slot == partner
         members = (jnp.where(in_last, partner, first), jnp.where(in_last, SLOTS - 1, second))
-        return members, jnp.where(in_last, 0, 1), jnp.where(jnp.logical_or(in_last, slot == first), 0, 1)
+        side = jnp.where(jnp.logical_or(in_last, slot == first), 0, 1)
+        return members, rotation_ref[jnp.where(in_last, 0, 1), :, span(side, width)]
 
     return [place(slot) for slot in pair_slots(chosen_ref[1])]
 
 
-def own_kernel(chosen_ref, gram_ref, split_ref, came_ref, rotation_ref, sums_ref, cross_ref, pair_ref):
-    width = sums_ref.shape[1]
+def products_with(met, came):
+    width = met[0].shape[0]
+    by_high = mul(jnp.concatenate([*met, came[0]], axis=0), came[0], NT)
+    by_low = mul(jnp.concatenate([met[0], came[0]], axis=0), came[1], NT)
+    twice = by_low[width:]
+    return by_high[:width] + (by_high[width:2 * width] + by_low[:width]), by_high[2 * width:] + (twice + twice.T)
+
+
+def meet_kernel(chosen_ref, gram_ref, split_ref, came_ref, rotation_ref, _, sums_ref, met_ref, cross_ref, pair_ref):
+    width = met_ref.shape[1]
+    half = came_ref.shape[1]
 
     def between(rows, others):
         return jnp.concatenate(
             [jnp.concatenate([gram_ref[span(r, width), span(c, width)] for c in others], axis=1) for r in rows], axis=0)
 
-    def squares(gram, turn):
-        return jnp.sum(turn * dot_split(gram, turn), axis=0, keepdims=True)
-
-    found = places(chosen_ref)
-    (meets_in, low_in, high_in), (meets_turn, low_turn, high_turn) = [members for members, _, _ in found], [
-        rotation_ref[pair, :, span(side, width)] for _, pair, side in found
-    ]
-    here = near(split_ref, meets_in, width)
-    came = halves(came_ref[...])
-    pair = 2 * width
-    by_high = mul(jnp.concatenate([*here, came[0]], axis=0), came[0], NT)
-    by_low = mul(jnp.concatenate([here[0], came[0]], axis=0), came[1], NT)
-    cross_ref[...] = by_high[:pair] + (by_high[pair:2 * pair] + by_low[:pair])
-    pair_ref[...] = by_high[2 * pair:] + (by_low[pair:] + by_low[pair:].T)
-    sums_ref[:width, :] = jnp.zeros((width, width), F32)
-    sums_ref[width:2 * width, :] = dot_split(low_turn, dot_split(between(low_in, high_in), high_turn), TN)
-    rows = [
-        squares(between(meets_in, meets_in), meets_turn),
-        jnp.zeros((1, width), F32),
-        squares(between(low_in, low_in), low_turn),
-        squares(between(high_in, high_in), high_turn),
-        jnp.zeros((4, width), F32),
-    ]
-    sums_ref[2 * width:, :] = jnp.concatenate(rows, axis=0)
-
-
-def own_sums(chosen, gram, split, came, turns):
-    width, rows = came.shape
-    return pl.pallas_call(
-        own_kernel,
-        in_specs=[SMEM] + [VMEM] * 4,
-        out_specs=[VMEM] * 3,
+    def squares(members, turn):
+        return jnp.sum(turn * dot_split(between(members, members), turn), axis=0, keepdims=True)
+
+    meets, low, high = places(chosen_ref, rotation_ref)
+    here = [jnp.concatenate([split_ref[span(m + start, width), :] for m in meets[0]], axis=0) for start in (0, SLOTS)]
+    met = halves(mul_split(halves(meets[1]), here, TN))
+    for term in range(2):
+        met_ref[term] = met[term]
+    sums_ref[:width, :] = dot_split(low[1], dot_split(between(low[0], high[0]), high[1]), TN)
+    sums_ref[width:, :] = jnp.concatenate(
+        [squares(*meets), jnp.zeros((1, width), F32), squares(*low), squares(*high), jnp.zeros((4, width), F32)], axis=0)
+    cross_ref[...], pair_ref[...] = products_with([part[:, :half] for part in met], halves(came_ref[...]))
+
+
+def meet(chosen, gram, split, came, turns, after):
+    pair, half = came.shape
+    width = pair // 2
+    return pl.pallas_call(
+        meet_kernel,
+        in_specs=[SMEM] + [VMEM] * 4 + [ANY],
+        out_specs=[VMEM] * 4,
         out_shape=[
-            jax.ShapeDtypeStruct((2 * width + 8, width), F32),
-            jax.ShapeDtypeStruct((2 * width, width), F32),
-            jax.ShapeDtypeStruct((width, width), F32),
+            jax.ShapeDtypeStruct((width + 8, width), F32),
+            jax.ShapeDtypeStruct((2, width, 2 * half), BF16),
+            jax.ShapeDtypeStruct((width, pair), F32),
+            jax.ShapeDtypeStruct((pair, pair), F32),
         ],
-        name="own_sums",
-        **params(16, 16 * width * width * rows, 24 * width * rows),
-    )(chosen, gram, split, came, turns)
-
-
-def cross_kernel(chosen_ref, split_ref, first_ref, second_ref, cross_ref, top_ref, rotation_ref, meets_ref, pair_ref):
-    width = first_ref.shape[0]
-    members, index, side = places(chosen_ref)[0]
-    turn = rotation_ref[index, :, span(side, width)]
-    here = near(split_ref, members, width)
-    first, second = halves(first_ref[...]), halves(second_ref[...])
-    pair = 2 * width
-    by_high = mul(jnp.concatenate([*here, *first, second[0]], axis=0), second[0], NT)
-    by_low = mul(jnp.concatenate([here[0], first[0], second[0]], axis=0), second[1], NT)
-    cross = by_high[:pair] + (by_high[pair:2 * pair] + by_low[:pair])
-    meets_ref[...] = dot_split(turn, jnp.concatenate([cross_ref[...], cross], axis=1), TN)
-    rest = by_high[2 * pair:]
-    mixed = rest[:width] + (rest[width:pair] + by_low[pair:pair + width])
-    twice = by_low[pair + width:]
-    pair_ref[:width, :width] = top_ref[...]
-    pair_ref[:width, width:] = mixed
-    pair_ref[width:, :width] = mixed.T
-    pair_ref[width:, width:] = rest[pair:] + (twice + twice.T)
-
-
-def came_sums(chosen, split, came, cross, top, turns):
-    width, rows = came[0].shape
-    return pl.pallas_call(
-        cross_kernel,
-        in_specs=[SMEM] + [VMEM] * 6,
-        out_specs=[VMEM] * 2,
-        out_shape=[
-            jax.ShapeDtypeStruct((width, 2 * width), F32),
-            jax.ShapeDtypeStruct((2 * width, 2 * width), F32),
-        ],
-        name="came_sums",
-        **params(16, 16 * width * width * rows, 28 * width * rows),
-    )(chosen, split, *came, cross, top, turns)
-
-
-def second_kernel(own_ref, meets_ref, pair_ref, turn_ref, sums_ref):
-    width = sums_ref.shape[1]
+        name="meet",
+        **params(16, 64 * width * width * half, 30 * width * half),
+    )(chosen, gram, split, came, turns, after)
+
+
+def came_kernel(met_ref, came_ref, cross_ref, pair_ref, turn_ref, own_ref, sums_ref):
+    width, half = met_ref.shape[1], came_ref.shape[1]
+    cross, pair = products_with([met_ref[term, :, half:] for term in range(2)], halves(came_ref[...]))
     turn = turn_ref[...]
     split = halves(turn)
-    sums_ref[...] = own_ref[...]
-    sums_ref[:width, :] = mul_split(halves(meets_ref[...]), split)
-    sums_ref[2 * width + 1:2 * width + 2, :] = jnp.sum(
-        turn * mul_split(halves(pair_ref[...]), split), axis=0, keepdims=True)
-
-
-def second_sums(own, meets, pair, came_turn):
-    return pl.pallas_call(
-        second_kernel,
-        in_specs=[VMEM] * 4,
+    sums_ref[:width, :] = mul_split(halves(cross + cross_ref[...]), split)
+    squares = jnp.sum(turn * mul_split(halves(pair + pair_ref[...]), split), axis=0, keepdims=True)
+    sums_ref[width:, :] = own_ref[...]
+    sums_ref[2 * width + 1:2 * width + 2, :] = squares
+
+
+def came_sums(met, came, cross, pair, came_turn, own):
+    width = met.shape[1]
+    return pl.pallas_call(
+        came_kernel,
+        in_specs=[VMEM] * 6,
         out_specs=VMEM,
-        out_shape=like(own)[0],
-        name="second_sums",
-        **params(8, 4 * pair.size * own.shape[1], 8 * pair.size),
-    )(own, meets, pair, came_turn)
-
-
-def picks(order_ref, rows):
-    order = order_ref[...]
-    return jnp.where(lax.broadcasted_iota(jnp.int32, (rows, order.shape[1]), 0) == order, 1.0, 0.0).astype(BF16)
-
-
-def order_kernel(order_ref, split_ref, value_ref, *refs):
+        out_shape=jax.ShapeDtypeStruct((2 * width + 8, width), F32),
+        name="came_sums",
+        **params(16, 32 * width * came.size, 12 * came.size),
+    )(met, came, cross, pair, came_turn, own)
+
+
+def picks_kernel(order_ref, value_ref, carried_ref, picks_ref):
+    rows = order_ref.shape[1]
+    carried_ref[...] = value_ref[...]
+    for start in range(0, rows, LANES):
+        here = slice(start, start + LANES)
+        place = jnp.broadcast_to(order_ref[:, here], (LANES, LANES)).T
+        for lane in range(0, rows, LANES):
+            lanes = lane + lax.broadcasted_iota(jnp.int32, (LANES, LANES), 1)
+            picks_ref[here, lane:lane + LANES] = jnp.where(place == lanes, 1.0, 0.0).astype(BF16)
+
+
+def picked(order, value):
+    rows = order.shape[1]
+    return pl.pallas_call(
+        picks_kernel,
+        in_specs=[VMEM] * 2,
+        out_specs=[VMEM] * 2,
+        out_shape=like(value) + [jax.ShapeDtypeStruct((rows, rows), BF16)],
+        name="picks",
+        **params(8, rows * rows, 2 * rows * rows),
+    )(order, value)
+
+
+def order_kernel(start, stop, picks_ref, split_ref, value_ref, *refs):
     carried_ref, matrix_ref = refs[-2:]
     width = matrix_ref.shape[3]
-
-    @pl.when(pl.program_id(0) == 0)
-    def _():
-        carried_ref[...] = value_ref[...]
-
-    both = mul(split_ref[...], picks(order_ref, split_ref.shape[1]))
+    carried_ref[...] = value_ref[...]
+    both = mul(picks_ref[start:stop, :], split_ref[...], NT)
     for term in range(2):
         for block in range(SLOTS):
-            start = (term * SLOTS + block) * width
-            matrix_ref[term, block] = both[start:start + width].T.astype(BF16)
-
-
-def ordered(order, split, value, tiles, into=None):
+            first = (term * SLOTS + block) * width
+            matrix_ref[term, block, start:stop, :] = both[:, first:first + width].astype(BF16)
+
+
+def ordered(picks, split, value, span_of, into=None):
     columns, rows = split.shape[0] // 2, split.shape[1]
-    width = columns // SLOTS
-    chunk = 2 * width
-    start, stop = tiles
     extra = () if into is None else (into,)
     return pl.pallas_call(
-        order_kernel,
-        grid=(stop - start,),
-        in_specs=[
-            pl.BlockSpec((1, chunk), lambda k: (0, k + start)),
-            VMEM,
-            VMEM,
-        ] + [ANY] * len(extra),
-        out_specs=[VMEM, pl.BlockSpec((2, SLOTS, chunk, width), lambda k: (0, 0, k + start, 0))],
-        out_shape=like(value) + [jax.ShapeDtypeStruct((2, SLOTS, rows, width), BF16)],
+        functools.partial(order_kernel, *span_of),
+        in_specs=[VMEM] * (3 + len(extra)),
+        out_specs=[VMEM] * 2,
+        out_shape=like(value) + [jax.ShapeDtypeStruct((2, SLOTS, rows, columns // SLOTS), BF16)],
         input_output_aliases={} if into is None else {3: 1},
         name="row_order",
-        **params(16, 4 * columns * rows * chunk * (stop - start), 8 * columns * rows),
-    )(order, split, value, *extra)
-
-
-def turn_kernel(chosen_ref, matrix_ref, rotation_ref, value_ref, carried_ref, turned_ref, meets_ref):
-    width = matrix_ref.shape[3]
+        **params(16, 4 * columns * rows * (span_of[1] - span_of[0]), 8 * columns * rows),
+    )(picks, split, value, *extra)
+
+
+def behind_kernel(chosen_ref, matrix_ref, rotation_ref, block_ref):
+    rows, width = block_ref.shape
+    (one, two), turn = places(chosen_ref, rotation_ref)[0]
+    high, low = halves(turn)
+    wide = jnp.concatenate([high, low], axis=1)
+    chunk = rows // PARTS
+    for part in range(PARTS):
+        here = pl.ds(part * chunk, chunk)
+        pair = [
+            jnp.concatenate([matrix_ref[term, one, here], matrix_ref[term, two, here]], axis=1) for term in range(2)
+        ]
+        both = mul(pair[0], wide)
+        block_ref[here] = both[:, :width] + (both[:, width:] + mul(pair[1], high))
+
+
+def behind_block(chosen, matrix, turns):
+    _, _, rows, width = matrix.shape
+    return pl.pallas_call(
+        behind_kernel,
+        in_specs=[SMEM] + [VMEM] * 2,
+        out_specs=VMEM,
+        out_shape=jax.ShapeDtypeStruct((rows, width), F32),
+        name="behind_block",
+        **params(16, 12 * rows * width * width, 2 * matrix.size),
+    )(chosen, matrix, turns)
+
+
+def turn_kernel(chosen_ref, matrix_ref, rotation_ref, value_ref, carried_ref, turned_ref):
+    rows, width = matrix_ref.shape[2:]
     partner, first, second = pair_slots(chosen_ref[0])
-
-    @pl.when(pl.program_id(0) == 0)
-    def _():
-        carried_ref[...] = value_ref[...]
-
+    carried_ref[...] = value_ref[...]
+    chunk = rows // PARTS
     for index, (one, two) in enumerate(((partner, SLOTS - 1), (first, second))):
-        pair = [jnp.concatenate([matrix_ref[term, one], matrix_ref[term, two]], axis=1) for term in range(2)]
-        turned = mul_split(pair, halves(rotation_ref[index]))
-        for term, part in enumerate(halves(turned)):
-            turned_ref[term, one] = part[:, :width]
-            turned_ref[term, two] = part[:, width:]
-    slot = 2 - chosen_ref[1]
-    meets_ref[...] = turned_ref[0, slot].astype(F32) + turned_ref[1, slot].astype(F32)
-
+        turn = halves(rotation_ref[index])
+        for part in range(PARTS):
+            here = pl.ds(part * chunk, chunk)
+            pair = [
+                jnp.concatenate([matrix_ref[term, one, here], matrix_ref[term, two, here]], axis=1) for term in range(2)
+            ]
+            for term, half in enumerate(halves(mul_split(pair, turn))):
+                turned_ref[term, one, here] = half[:, :width]
+                turned_ref[term, two, here] = half[:, width:]
 
 def turn(chosen, matrix, turns, value):
     _, _, rows, width = matrix.shape
-    chunk = rows // 2
-    blocks = pl.BlockSpec((2, SLOTS, chunk, width), lambda k: (0, 0, k, 0))
     return pl.pallas_call(
         turn_kernel,
-        grid=(rows // chunk,),
-        in_specs=[SMEM, blocks, VMEM, VMEM],
-        out_specs=[VMEM, blocks, pl.BlockSpec((chunk, width), lambda k: (k, 0))],
-        out_shape=like(value, matrix) + [jax.ShapeDtypeStruct((rows, width), F32)],
+        in_specs=[SMEM] + [VMEM] * 3,
+        out_specs=[VMEM] * 2,
+        out_shape=like(value, matrix),
         name="first_turn",
-        **params(20, 24 * rows * width * width, 4 * matrix.size),
+        **params(16, 24 * rows * width * width, 4 * matrix.size),
     )(chosen, matrix, turns, value)
 
 
-def moved_kernel(order_ref, one_ref, two_ref, turn_ref, value_ref, carried_ref, block_ref, split_ref):
+def moved_kernel(picks_ref, one_ref, two_ref, turn_ref, value_ref, carried_ref, block_ref):
     width = block_ref.shape[2]
-    rows = one_ref.shape[1]
-
-    @pl.when(pl.program_id(0) == 0)
-    def _():
-        carried_ref[...] = value_ref[...]
-        high, low = halves(
-            dot_split(turn_ref[...], jnp.concatenate([one_ref[...], two_ref[...]], axis=0), TN))
-        split_ref[:width, :] = high
-        split_ref[width:, :] = low
-
-    both = mul(split_ref[...], picks(order_ref, rows))
+    carried_ref[...] = value_ref[...]
+    came = jnp.concatenate([one_ref[...], two_ref[...]], axis=1)
+    both = mul(picks_ref[...], jnp.concatenate(halves(dot_split(turn_ref[...], came, TN)), axis=0), NT)
     for term in range(2):
-        block_ref[term] = both[term * width:(term + 1) * width].T.astype(BF16)
-
-
-def moved_block(order, came, came_turn, value):
-    width, rows = came[0].shape
-    pair = chunk = 2 * width
+        block_ref[term] = both[:, term * width:(term + 1) * width].astype(BF16)
+
+
+def moved_block(picks, came, came_turn, value):
+    rows = picks.shape[0]
+    pair, width = came_turn.shape
     return pl.pallas_call(
         moved_kernel,
-        grid=(rows // chunk,),
-        in_specs=[
-            pl.BlockSpec((1, chunk), lambda k: (0, k)),
-            VMEM,
-            VMEM,
-            VMEM,
-            VMEM,
-        ],
-        out_specs=[VMEM, pl.BlockSpec((2, chunk, width), lambda k: (0, k, 0))],
+        in_specs=[VMEM] * 5,
+        out_specs=[VMEM] * 2,
         out_shape=like(value) + [jax.ShapeDtypeStruct((2, rows, width), BF16)],
-        scratch_shapes=[pltpu.VMEM((pair, rows), BF16)],
         name="moved_block",
-        **params(16, 4 * width * rows * rows, 8 * pair * rows),
-    )(order, *came, came_turn, value)
+        **params(16, 4 * width * rows * rows, 2 * picks.size),
+    )(picks, *came, came_turn, value)
 
 
 def most_kernel(chosen_ref, turned_ref, moved_ref, rotation_ref, out_ref, ready_ref, sems):
@@ -640,7 +623,7 @@
     held = arrived.reshape(-1, row_count)
     order = (pixel_order - lax.axis_index("rows") * row_count).reshape(1, row_count)
     chosen = lax.dynamic_index_in_dim(pairing, lax.axis_index("cols"), axis=1, keepdims=False)
-    chunks = row_count // (held.shape[0] // 2)
+    part = row_count * 3 // 8
     kept = {}
 
     def gram_work(value):
@@ -648,38 +631,35 @@
         return value
 
     def order_first(value):
-        value, kept["matrix"] = ordered(order, kept["split"], value, (0, chunks * 3 // 8))
+        value, kept["picks"] = picked(order, value)
+        value, kept["matrix"] = ordered(kept["picks"], kept["split"], value, (0, part))
         return value
 
     def order_rest(value):
-        value, kept["matrix"] = ordered(order, kept["split"], value, (chunks * 3 // 8, chunks), kept["matrix"])
+        value, kept["matrix"] = ordered(kept["picks"], kept["split"], value, (part, row_count), kept["matrix"])
         return value
 
     def turn_work(value):
-        value, kept["turned"], kept["meets"] = turn(chosen, kept["matrix"], turns, value)
+        value, kept["turned"] = turn(chosen, kept["matrix"], turns, value)
         return value
 
-    def taken_work(value):
-        value, meets = lax.optimization_barrier((value, kept["meets"]))
-        kept["behind"] = from_behind(meets, "cols", -1)
+    def moved_work(value):
+        value, kept["moved"] = moved_block(kept["picks"], came, came_turn, value)
         return value
 
-    def moved_work(value):
-        value, kept["moved"] = moved_block(order, came, came_turn, value)
-        return value
-
     sums, *last, tiles = couplings(chosen, held)
-    came = [from_behind(block, "cols", 1) for block in last]
+    came = [from_behind(half, "cols", 1) for half in last]
     turns, sent = two_rotations(*summed(sums, "rows", [gram_work, order_first, order_rest]))
     came_turn = from_behind(sent, "cols", 1)
-    own, cross, top = own_sums(chosen, kept["gram"], kept["split"], came[0], turns)
-    meets, pair = came_sums(chosen, kept["split"], came, cross, top, turns)
-    sums = second_sums(own, meets, pair, came_turn)
-
-    second_turns, sent = two_rotations(*summed(sums, "rows", [turn_work, taken_work, moved_work]))
+    behind_sent = behind_block(chosen, kept["matrix"], turns)
+    behind = from_behind(behind_sent, "cols", -1)
+    own, met, cross, pair = meet(chosen, kept["gram"], kept["split"], came[0], turns, behind_sent)
+    sums = came_sums(met, came[1], cross, pair, came_turn, own)
+
+    second_turns, sent = two_rotations(*summed(sums, "rows", [turn_work, moved_work]))
     behind_turn = from_behind(sent, "cols", -1)
     out = most_slots(chosen, kept["turned"], kept["moved"], second_turns)
-    return last_slot(kept["turned"], kept["behind"], behind_turn, out)
+    return last_slot(kept["turned"], behind, behind_turn, out)
 
 
 def solution(mesh):

time: 167 us -> 165 us (0.988)
  starting transfers between devices: 17.9 us -> 21.9 us
  waiting for transfers between devices: 103 us -> 99.8 us
  Pallas kernels: 44.8 us -> 42.1 us
    ppermute x5, starting transfers between devices: 6.56 us -> 9.55 us  [from_behind(): return lax.ppermute(value, axis, pairs)]
    pallas_call x7 -> x8, Pallas kernels: 24.4 us -> 21.4 us  [the longest x2 9.14 us: ordered(): pl.pallas_call(functools.partial(order_kernel, *span_of), in_specs=[VMEM]...]
    ppermute x6, waiting for transfers between devices: 8.51 us -> 6.7 us  [summed(): lax.ppermute(value, axis, [(source, source ^ distance) for source in rang...]
    ppermute x5, waiting for transfers between devices: 1.82 us -> 0.01 us  [from_behind(): return lax.ppermute(value, axis, pairs)]
  transfers between devices with their start and end apart: 12 -> 12, of which waited for: 7 -> 5; matrix products, arithmetic and copies ran while one was open for 0% -> 0% of each run, Pallas kernels for 22% -> 20%
where the time goes in v2:
time: 165 us
  waiting for transfers between devices  99.8 us (60%)
  Pallas kernels  42.1 us (26%)
  starting transfers between devices  21.9 us (13%)
    all_to_all x1, waiting for transfers between devices, body(): lax.all_to_all(pieces, ('rows', 'cols'), split_axis=0, concat_axis=0, til...  93.1 us
    ppermute x5, starting transfers between devices, from_behind(): return lax.ppermute(value, axis, pairs)  9.55 us
    pallas_call x2, Pallas kernels, ordered(): pl.pallas_call(functools.partial(order_kernel, *span_of), in_specs=[VMEM]...  9.14 us
    all_to_all x1, starting transfers between devices, body(): lax.all_to_all(pieces, ('rows', 'cols'), split_axis=0, concat_axis=0, til...  7.16 us
    ppermute x6, waiting for transfers between devices, summed(): lax.ppermute(value, axis, [(source, source ^ distance) for source in rang...  6.7 us
    pallas_call x2, Pallas kernels, two_rotations(): pl.pallas_call(rotation_kernel, in_specs=[VMEM] * 2, out_specs=[VMEM] * 2...  6.33 us
    ppermute x6, starting transfers between devices, summed(): lax.ppermute(value, axis, [(source, source ^ distance) for source in rang...  5.21 us
    pallas_call x1, Pallas kernels, spread(): pl.pallas_call(spread_kernel, in_specs=[ANY], out_specs=HBM, out_shape=ja...  3.49 us
  transfers between devices with their start and end apart: 12, of which 5 were waited for; matrix products, arithmetic and copies ran while one was open for 0% of the time, Pallas kernels for 20%

profile of v2, /device:TPU:1, one launch (start us, length us, event | category | flops | bytes accessed | tf_op | source)
XLA Modules:
  0.0 164.5 jit_solution(2024928311263231925)
XLA Ops:
  0.0 0.0 copy-start
  0.0 3.5 %spread.1 = f32[8,4,16,2048]{3,2,1,0:T(8,128)} custom-call(f32[32,2,16384]{2,1,0:T(2,128)} %tracks_ref.1), custom_call_target="tpu_custom_call" | custom-call | bytes 8388608 | tf_op jit(solution)/shard_map/spread/pallas_call | solution.py:108
  3.5 0.0 copy-start.1
  3.5 7.2 %all-to-all-start = ((f32[32,16,2048]{2,1,0:T(8,128)}), f32[32,16,2048]{2,1,0:T(8,128)}, u32[]{:S(2)}, u32[]{:S(2)}) async-start(f32[32,16,2048]{2,1,0:T(8,128)} %bitcast.4), calls=%async_computation | async-start | bytes 8388608 | tf_op jit(solution)/shard_map/all_to_all | solution.py:622
  10.7 0.0 copy-done
  10.7 0.2 dynamic-slice_reduce_fusion.chosen_ref
  10.9 0.0 copy-done.1
  10.9 93.1 %all-to-all-done = f32[32,16,2048]{2,1,0:T(8,128)} async-done(((f32[32,16,2048]{2,1,0:T(8,128)}), f32[32,16,2048]{2,1,0:T(8,128)}, u32[]{:S(2)}, u32[]{:S(2)}) %all-to-all-start) | async-done | bytes 4194336 | tf_op jit(solution)/shard_map/all_to_all | solution.py:622
  104.0 3.4 %couplings.1 = (f32[264,128]{1,0:T(8,128)S(1)}, f32[256,1024]{1,0:T(8,128)S(1)}, f32[256,1024]{1,0:T(8,128)S(1)}, f32[16,512,128]{2,1,0:T(8,128)S(1)}) custom-call(s32[2]{0:T(128)S(1)} %dynamic-slice_reduce_fusion.chosen_ref, f32[512,2048]{1,0:T(8,128)} %bitcast.2.held_ref), custom_call_target="tpu_custom_call" | custom-call | flops 536870912 | bytes 6291456 | tf_op jit(solution)/shard_map/couplings/pallas_call | solution.py:163
  107.4 1.0 collective-permute-start
  108.4 2.5 %collective-permute-start.3 = (f32[256,1024]{1,0:T(8,128)S(1)}, f32[256,1024]{1,0:T(8,128)S(1)}, u32[]{:S(2)}, u32[]{:S(2)}) collective-permute-start(f32[256,1024]{1,0:T(8,128)S(1)} %get-tuple-element.42), channel_id=1, source_target_pairs={{0,1},{1,2},{2,3},{3,0},{4,5},{5,6},{6,7},{7,4},{8,9},{9,10},{10,1... | collective-permute-start | bytes 3145736 | tf_op jit(solution)/shard_map/ppermute | solution.py:596
  110.9 0.0 collective-permute-start.4
  110.9 2.6 %gram.1 = (f32[264,128]{1,0:T(8,128)S(1)}, f32[512,512]{1,0:T(8,128)S(1)}, bf16[1024,2048]{1,0:T(8,128)(2,1)S(1)}) custom-call(f32[264,128]{1,0:T(8,128)S(1)} %get-tuple-element.30.value_ref, f32[16,512,128]{2,1,0:T(8,128)S(1)} %get-tuple-element.31.came_ref), custom_call_target="tpu_custom_call" | custom-call | flops 2147483648 | bytes 8388608 | tf_op jit(solution)/shard_map/gram/pallas_call | solution.py:205
  113.5 0.0 collective-permute-done
  113.6 0.1 collective-permute-start.1
  113.6 1.7 %picks.1 = (f32[264,128]{1,0:T(8,128)S(1)}, bf16[2048,2048]{1,0:T(8,128)(2,1)S(1)}) custom-call(s32[1,2048]{1,0:T(1,128)S(1)} %bitcast.3, f32[264,128]{1,0:T(8,128)S(1)} %add.17.value_ref), custom_call_target="tpu_custom_call" | custom-call | flops 4194304 | bytes 8388608 | tf_op jit(solution)/shard_map/picks/pallas_call | solution.py:407
  115.3 3.5 %row_order.2 = (f32[264,128]{1,0:T(8,128)S(1)}, bf16[2,4,2048,128]{3,2,1,0:T(8,128)(2,1)S(1)}) custom-call(bf16[2048,2048]{1,0:T(8,128)(2,1)S(1)} %get-tuple-element.33.picks_ref, bf16[1024,2048]{1,0:T(8,128)(2,1)S(1)} %get-tuple-element.34.split_ref, f32[264,128]{1,0:T(8,128)S(1)} %get-tuple-element.35.value_ref), custom_call_target="tpu_custom_call" | custom-call | flops 3221225472 | bytes 8388608 | tf_op jit(solution)/shard_map/row_order/pallas_call | solution.py:431
  118.8 0.0 collective-permute-done.1
  118.8 1.8 %collective-permute-start.2 = (f32[264,128]{1,0:T(8,128)S(1)}, f32[264,128]{1,0:T(8,128)S(1)}, u32[]{:S(2)}, u32[]{:S(2)}) collective-permute-start(f32[264,128]{1,0:T(8,128)S(1)} %add.18.value_ref), channel_id=1, source_target_pairs={{0,16},{4,20},{8,24},{12,28},{16,0},{20,4},{24,8},{28,12},{1,17},{... | collective-permute-start | bytes 405512 | tf_op jit(solution)/shard_map/ppermute | solution.py:608
  120.6 5.7 %row_order.3 = (f32[264,128]{1,0:T(8,128)S(1)}, bf16[2,4,2048,128]{3,2,1,0:T(8,128)(2,1)S(1)}) custom-call(bf16[2048,2048]{1,0:T(8,128)(2,1)S(1)} %get-tuple-element.33.picks_ref, bf16[1024,2048]{1,0:T(8,128)(2,1)S(1)} %get-tuple-element.34.split_ref, f32[264,128]{1,0:T(8,128)S(1)} %add.18.value_ref, ...), custom_call_target="tpu_custom_call", output_to_operand_aliasing={{1}: (3, {})} | custom-call | flops 5368709120 | bytes 8388608 | tf_op jit(solution)/shard_map/row_order/pallas_call | solution.py:431
  126.3 0.6 collective-permute-done.2.two_ref
  127.0 3.3 %rotations.2 = (f32[2,256,256]{2,1,0:T(8,128)S(1)}, f32[256,128]{1,0:T(8,128)S(1)}) custom-call(f32[264,128]{1,0:T(8,128)S(1)} %get-tuple-element.39.one_ref, f32[264,128]{1,0:T(8,128)S(1)} %collective-permute-done.2.two_ref), custom_call_target="tpu_custom_call" | custom-call | flops 2516582400 | bytes 262144 | tf_op jit(solution)/shard_map/rotations/pallas_call | solution.py:297
  130.3 1.6 collective-permute-start.5
  131.9 1.2 behind_block.1._
  133.2 0.2 collective-permute-start.6
  133.3 0.0 collective-permute-done.3.came_ref.one_ref
  133.4 2.4 %meet.1 = (f32[136,128]{1,0:T(8,128)S(1)}, bf16[2,128,2048]{2,1,0:T(8,128)(2,1)S(1)}, f32[128,256]{1,0:T(8,128)S(1)}, f32[256,256]{1,0:T(8,128)S(1)}) custom-call(s32[2]{0:T(128)S(1)} %dynamic-slice_reduce_fusion.chosen_ref, f32[512,512]{1,0:T(8,128)S(1)} %get-tuple-element.41.gram_ref, bf16[1024,2048]{1,0:T(8,128)(2,1)S(1)} %get-tuple-element.34.split_ref, ...), custom_call_target="tpu_custom_call" | custom-call | flops 1073741824 | bytes 3932160 | tf_op jit(solution)/shard_map/meet/pallas_call | solution.py:356
  135.8 0.0 collective-permute-done.5.turn_ref
  135.8 0.0 collective-permute-done.4.came_ref.two_ref
  135.8 1.2 came_sums.1.value_ref
  137.0 0.9 collective-permute-start.7
  137.9 2.5 %first_turn.1 = (f32[264,128]{1,0:T(8,128)S(1)}, bf16[2,4,2048,128]{3,2,1,0:T(8,128)(2,1)S(1)}) custom-call(s32[2]{0:T(128)S(1)} %dynamic-slice_reduce_fusion.chosen_ref, bf16[2,4,2048,128]{3,2,1,0:T(8,128)(2,1)S(1)} %get-tuple-element.38.matrix_ref, f32[2,256,256]{2,1,0:T(8,128)S(1)} %get-tuple-element.40.rotation_ref, f32[264,128]{1,0:T(8,128)S(1)} %came_sums.1.value_ref), custom_call_target="tpu_custom_call" | custom-call | flops 805306368 | bytes 8388608 | tf_op jit(solution)/shard_map/first_turn/pallas_call | solution.py:487
  140.5 0.4 collective-permute-done.7
  141.0 0.1 collective-permute-start.8
  141.0 3.2 %moved_block.1 = (f32[264,128]{1,0:T(8,128)S(1)}, bf16[2,2048,128]{2,1,0:T(8,128)(2,1)S(1)}) custom-call(bf16[2048,2048]{1,0:T(8,128)(2,1)S(1)} %get-tuple-element.33.picks_ref, f32[256,1024]{1,0:T(8,128)S(1)} %collective-permute-done.3.came_ref.one_ref, f32[256,1024]{1,0:T(8,128)S(1)} %collective-permute-done.4.came_ref.two_ref, ...), custom_call_target="tpu_custom_call" | custom-call | flops 2147483648 | bytes 8388608 | tf_op jit(solution)/shard_map/moved_block/pallas_call | solution.py:509
  144.2 0.7 collective-permute-done.8
  144.9 1.3 collective-permute-start.9
  146.2 4.9 %collective-permute-done.9.two_ref = f32[264,128]{1,0:T(8,128)S(1)} collective-permute-done((f32[264,128]{1,0:T(8,128)S(1)}, f32[264,128]{1,0:T(8,128)S(1)}, u32[]{:S(2)}, u32[]{:S(2)}) %collective-permute-start.9) | collective-permute-done | bytes 135200 | tf_op jit(solution)/shard_map/ppermute | solution.py:608
  151.2 3.1 %rotations.3 = (f32[2,256,256]{2,1,0:T(8,128)S(1)}, f32[256,128]{1,0:T(8,128)S(1)}) custom-call(f32[264,128]{1,0:T(8,128)S(1)} %add.20.one_ref, f32[264,128]{1,0:T(8,128)S(1)} %collective-permute-done.9.two_ref), custom_call_target="tpu_custom_call" | custom-call | flops 2516582400 | bytes 262144 | tf_op jit(solution)/shard_map/rotations/pallas_call | solution.py:297
  154.2 5.2 %collective-permute-start.10 = (f32[256,128]{1,0:T(8,128)S(1)}, f32[256,128]{1,0:T(8,128)S(1)}, u32[]{:S(2)}, u32[]{:S(2)}) collective-permute-start(f32[256,128]{1,0:T(8,128)S(1)} %get-tuple-element.52), channel_id=1, source_target_pairs={{0,3},{1,0},{2,1},{3,2},{4,7},{5,4},{6,5},{7,6},{8,11},{9,8},{10,9... | collective-permute-start | bytes 393224 | tf_op jit(solution)/shard_map/ppermute | solution.py:596
  159.4 3.2 %second_turn.1._ = f32[2048,512]{1,0:T(8,128)} custom-call(s32[2]{0:T(128)S(1)} %dynamic-slice_reduce_fusion.chosen_ref, bf16[2,4,2048,128]{3,2,1,0:T(8,128)(2,1)S(1)} %get-tuple-element.49.turned_ref, bf16[2,2048,128]{2,1,0:T(8,128)(2,1)S(1)} %get-tuple-element.53.moved_ref, f32[2,256,256]{2,1,0:T(8,128)S(1)} %get-tuple-element.54.rotation_ref), custom_call_target="tpu_custom_call" | custom-call | flops 603979776 | bytes 8388608 | tf_op jit(solution)/shard_map/second_turn/pallas_call | solution.py:549
  162.6 0.0 collective-permute-done.6.behind_ref
  162.6 0.0 collective-permute-done.10.turn_ref
  162.6 1.7 %last_slot.1 = f32[2048,512]{1,0:T(8,128)} custom-call(bf16[2,4,2048,128]{3,2,1,0:T(8,128)(2,1)S(1)} %get-tuple-element.49.turned_ref, f32[2048,128]{1,0:T(8,128)S(1)} %collective-permute-done.6.behind_ref, f32[256,128]{1,0:T(8,128)S(1)} %collective-permute-done.10.turn_ref, f32[2048,512]{1,0:T(8,128)} %second_turn.1._), custom_call_target="tpu_custom_call", output_to_operand_aliasing={{}: (3, {})} | custom-call | flops 402653184 | bytes 3145728 | tf_op jit(solution)/shard_map/last_slot/pallas_call | solution.py:581
  (5 shorter events, 0.1 us)
Async XLA Ops:
  0.0 10.7 %copy-start = (s32[2,4]{1,0:T(2,128)S(1)}, s32[2,4]{1,0:T(2,128)}, u32[]{:S(2)}) copy-start(s32[2,4]{1,0:T(2,128)} %param.5) | copy-start | bytes 100
  3.5 7.4 %copy-start.1 = (s32[2048]{0:T(1024)S(1)}, s32[2048]{0:T(1024)}, u32[]{:S(2)}) copy-start(s32[2048]{0:T(1024)} %param.4) | copy-start | bytes 24580
  3.5 100.5 %all-to-all-start = ((f32[32,16,2048]{2,1,0:T(8,128)}), f32[32,16,2048]{2,1,0:T(8,128)}, u32[]{:S(2)}, u32[]{:S(2)}) async-start(f32[32,16,2048]{2,1,0:T(8,128)} %bitcast.4), calls=%async_computation | async-start | bytes 8388608 | tf_op jit(solution)/shard_map/all_to_all | solution.py:622
  107.4 6.1 %collective-permute-start = (f32[264,128]{1,0:T(8,128)S(1)}, f32[264,128]{1,0:T(8,128)S(1)}, u32[]{:S(2)}, u32[]{:S(2)}) collective-permute-start(f32[264,128]{1,0:T(8,128)S(1)} %get-tuple-element.30.value_ref), channel_id=1, source_target_pairs={{0,4},{4,0},{8,12},{12,8},{16,20},{20,16},{24,28},{28,24},{1,5},{5... | collective-permute-start | bytes 405512 | tf_op jit(solution)/shard_map/ppermute | solution.py:608
  108.4 25.0 %collective-permute-start.3 = (f32[256,1024]{1,0:T(8,128)S(1)}, f32[256,1024]{1,0:T(8,128)S(1)}, u32[]{:S(2)}, u32[]{:S(2)}) collective-permute-start(f32[256,1024]{1,0:T(8,128)S(1)} %get-tuple-element.42), channel_id=1, source_target_pairs={{0,1},{1,2},{2,3},{3,0},{4,5},{5,6},{6,7},{7,4},{8,9},{9,10},{10,1... | collective-permute-start | bytes 3145736 | tf_op jit(solution)/shard_map/ppermute | solution.py:596
  110.9 24.9 %collective-permute-start.4 = (f32[256,1024]{1,0:T(8,128)S(1)}, f32[256,1024]{1,0:T(8,128)S(1)}, u32[]{:S(2)}, u32[]{:S(2)}) collective-permute-start(f32[256,1024]{1,0:T(8,128)S(1)} %get-tuple-element.44), channel_id=1, source_target_pairs={{0,1},{1,2},{2,3},{3,0},{4,5},{5,6},{6,7},{7,4},{8,9},{9,10},{10,1... | collective-permute-start | bytes 3145736 | tf_op jit(solution)/shard_map/ppermute | solution.py:596
  113.6 5.2 %collective-permute-start.1 = (f32[264,128]{1,0:T(8,128)S(1)}, f32[264,128]{1,0:T(8,128)S(1)}, u32[]{:S(2)}, u32[]{:S(2)}) collective-permute-start(f32[264,128]{1,0:T(8,128)S(1)} %add.17.value_ref), channel_id=1, source_target_pairs={{0,8},{4,12},{8,0},{12,4},{16,24},{20,28},{24,16},{28,20},{1,9},{5... | collective-permute-start | bytes 405512 | tf_op jit(solution)/shard_map/ppermute | solution.py:608
  118.8 8.2 %collective-permute-start.2 = (f32[264,128]{1,0:T(8,128)S(1)}, f32[264,128]{1,0:T(8,128)S(1)}, u32[]{:S(2)}, u32[]{:S(2)}) collective-permute-start(f32[264,128]{1,0:T(8,128)S(1)} %add.18.value_ref), channel_id=1, source_target_pairs={{0,16},{4,20},{8,24},{12,28},{16,0},{20,4},{24,8},{28,12},{1,17},{... | collective-permute-start | bytes 405512 | tf_op jit(solution)/shard_map/ppermute | solution.py:608
  130.3 5.5 %collective-permute-start.5 = (f32[256,128]{1,0:T(8,128)S(1)}, f32[256,128]{1,0:T(8,128)S(1)}, u32[]{:S(2)}, u32[]{:S(2)}) collective-permute-start(f32[256,128]{1,0:T(8,128)S(1)} %get-tuple-element.47), channel_id=1, source_target_pairs={{0,1},{1,2},{2,3},{3,0},{4,5},{5,6},{6,7},{7,4},{8,9},{9,10},{10,1... | collective-permute-start | bytes 393224 | tf_op jit(solution)/shard_map/ppermute | solution.py:596
  133.2 29.4 %collective-permute-start.6 = (f32[2048,128]{1,0:T(8,128)S(1)}, f32[2048,128]{1,0:T(8,128)S(1)}, u32[]{:S(2)}, u32[]{:S(2)}) collective-permute-start(f32[2048,128]{1,0:T(8,128)S(1)} %behind_block.1._), channel_id=1, source_target_pairs={{0,3},{1,0},{2,1},{3,2},{4,7},{5,4},{6,5},{7,6},{8,11},{9,8},{10,9... | collective-permute-start | bytes 3145736 | tf_op jit(solution)/shard_map/ppermute | solution.py:596
  137.0 3.9 %collective-permute-start.7 = (f32[264,128]{1,0:T(8,128)S(1)}, f32[264,128]{1,0:T(8,128)S(1)}, u32[]{:S(2)}, u32[]{:S(2)}) collective-permute-start(f32[264,128]{1,0:T(8,128)S(1)} %came_sums.1.value_ref), channel_id=1, source_target_pairs={{0,4},{4,0},{8,12},{12,8},{16,20},{20,16},{24,28},{28,24},{1,5},{5... | collective-permute-start | bytes 405512 | tf_op jit(solution)/shard_map/ppermute | solution.py:608
  141.0 3.9 %collective-permute-start.8 = (f32[264,128]{1,0:T(8,128)S(1)}, f32[264,128]{1,0:T(8,128)S(1)}, u32[]{:S(2)}, u32[]{:S(2)}) collective-permute-start(f32[264,128]{1,0:T(8,128)S(1)} %add.19.value_ref), channel_id=1, source_target_pairs={{0,8},{4,12},{8,0},{12,4},{16,24},{20,28},{24,16},{28,20},{1,9},{5... | collective-permute-start | bytes 405512 | tf_op jit(solution)/shard_map/ppermute | solution.py:608
  144.9 6.3 %collective-permute-start.9 = (f32[264,128]{1,0:T(8,128)S(1)}, f32[264,128]{1,0:T(8,128)S(1)}, u32[]{:S(2)}, u32[]{:S(2)}) collective-permute-start(f32[264,128]{1,0:T(8,128)S(1)} %add.20.one_ref), channel_id=1, source_target_pairs={{0,16},{4,20},{8,24},{12,28},{16,0},{20,4},{24,8},{28,12},{1,17},{... | collective-permute-start | bytes 405512 | tf_op jit(solution)/shard_map/ppermute | solution.py:608
  154.2 8.4 %collective-permute-start.10 = (f32[256,128]{1,0:T(8,128)S(1)}, f32[256,128]{1,0:T(8,128)S(1)}, u32[]{:S(2)}, u32[]{:S(2)}) collective-permute-start(f32[256,128]{1,0:T(8,128)S(1)} %get-tuple-element.52), channel_id=1, source_target_pairs={{0,3},{1,0},{2,1},{3,2},{4,7},{5,4},{6,5},{7,6},{8,11},{9,8},{10,9... | collective-permute-start | bytes 393224 | tf_op jit(solution)/shard_map/ppermute | solution.py:596

commit v3 on v2

--- a/solution.py
+++ b/solution.py
@@ -63,6 +63,12 @@
 
 def mul_split(a, b, dims=NN):
     return mul(a[0], b[0], dims) + (mul(a[0], b[1], dims) + mul(a[1], b[0], dims))
+
+
+def mul_narrow(a, b):
+    width = b[0].shape[1]
+    both = mul(a[0], jnp.concatenate(b, axis=1))
+    return both[:, :width] + (both[:, width:] + mul(a[1], b[0]))
 
 
 def dot_split(a, b, dims=NN):
@@ -292,11 +298,18 @@
         [(total[:width], sums[0:1], sums[1:2]), (total[width:2 * width], sums[2:3], sums[3:4])], rotation_ref, sent_ref)
 
 
-def two_rotations(one, two):
-    width = one.shape[1]
-    return pl.pallas_call(
-        rotation_kernel,
-        in_specs=[VMEM] * 2,
+def later_kernel(one_ref, one_got_ref, two_ref, two_got_ref, rotation_ref, sent_ref):
+    width = one_ref.shape[1]
+    totals = one_ref[...] + one_got_ref[...], two_ref[...] + two_got_ref[...]
+    put_rotations(
+        [(total[:width], total[width:width + 1], total[width + 1:width + 2]) for total in totals], rotation_ref, sent_ref)
+
+
+def two_rotations(*terms):
+    width = terms[0].shape[1]
+    return pl.pallas_call(
+        rotation_kernel if len(terms) == 2 else later_kernel,
+        in_specs=[VMEM] * len(terms),
         out_specs=[VMEM] * 2,
         out_shape=[
             jax.ShapeDtypeStruct((2, 2 * width, 2 * width), F32),
@@ -304,7 +317,7 @@
         ],
         name="rotations",
         **params(16, 300 * 4 * width**3, 16 * width * width),
-    )(one, two)
+    )(*terms)
 
 
 def places(chosen_ref, rotation_ref):
@@ -341,12 +354,14 @@
 
     meets, low, high = places(chosen_ref, rotation_ref)
     here = [jnp.concatenate([split_ref[span(m + start, width), :] for m in meets[0]], axis=0) for start in (0, SLOTS)]
-    met = halves(mul_split(halves(meets[1]), here, TN))
+    turn = halves(meets[1])
+    both = mul(jnp.concatenate(turn, axis=1), here[0], TN)
+    met = halves(both[:width] + (both[width:] + mul(turn[0], here[1], TN)))
     for term in range(2):
         met_ref[term] = met[term]
     sums_ref[:width, :] = dot_split(low[1], dot_split(between(low[0], high[0]), high[1]), TN)
     sums_ref[width:, :] = jnp.concatenate(
-        [squares(*meets), jnp.zeros((1, width), F32), squares(*low), squares(*high), jnp.zeros((4, width), F32)], axis=0)
+        [squares(*low), squares(*high), squares(*meets), jnp.zeros((5, width), F32)], axis=0)
     cross_ref[...], pair_ref[...] = products_with([part[:, :half] for part in met], halves(came_ref[...]))
 
 
@@ -375,8 +390,7 @@
     split = halves(turn)
     sums_ref[:width, :] = mul_split(halves(cross + cross_ref[...]), split)
     squares = jnp.sum(turn * mul_split(halves(pair + pair_ref[...]), split), axis=0, keepdims=True)
-    sums_ref[width:, :] = own_ref[...]
-    sums_ref[2 * width + 1:2 * width + 2, :] = squares
+    sums_ref[width:, :] = jnp.concatenate([own_ref[width + 2:width + 3], squares, jnp.zeros((6, width), F32)], axis=0)
 
 
 def came_sums(met, came, cross, pair, came_turn, own):
@@ -385,7 +399,7 @@
         came_kernel,
         in_specs=[VMEM] * 6,
         out_specs=VMEM,
-        out_shape=jax.ShapeDtypeStruct((2 * width + 8, width), F32),
+        out_shape=jax.ShapeDtypeStruct((width + 8, width), F32),
         name="came_sums",
         **params(16, 32 * width * came.size, 12 * came.size),
     )(met, came, cross, pair, came_turn, own)
@@ -442,16 +456,14 @@
 def behind_kernel(chosen_ref, matrix_ref, rotation_ref, block_ref):
     rows, width = block_ref.shape
     (one, two), turn = places(chosen_ref, rotation_ref)[0]
-    high, low = halves(turn)
-    wide = jnp.concatenate([high, low], axis=1)
+    turn = halves(turn)
     chunk = rows // PARTS
     for part in range(PARTS):
         here = pl.ds(part * chunk, chunk)
         pair = [
             jnp.concatenate([matrix_ref[term, one, here], matrix_ref[term, two, here]], axis=1) for term in range(2)
         ]
-        both = mul(pair[0], wide)
-        block_ref[here] = both[:, :width] + (both[:, width:] + mul(pair[1], high))
+        block_ref[here] = mul_narrow(pair, turn)
 
 
 def behind_block(chosen, matrix, turns):
@@ -535,7 +547,7 @@
         pair = mul_split(beside(block(low), block(high)), pair_turn)
         ready_ref[here, span(low, width)] = pair[:, :width]
         ready_ref[here, span(high, width)] = pair[:, width:]
-        ready_ref[here, span(meets, width)] = mul_split(
+        ready_ref[here, span(meets, width)] = mul_narrow(
             beside(block(meets), [moved_ref[term, here] for term in range(2)]), meets_turn)
         stores.append(pltpu.make_async_copy(
             ready_ref.at[here], out_ref.at[here, pl.ds(0, (SLOTS - 1) * width)], sems.at[part]))
@@ -568,7 +580,7 @@
             jnp.concatenate([one, turned_ref[term, SLOTS - 1, here]], axis=1)
             for term, one in enumerate(halves(behind_ref[here]))
         ]
-        ready_ref[here] = mul_split(pair, split)
+        ready_ref[here] = mul_narrow(pair, split)
         stores.append(pltpu.make_async_copy(
             ready_ref.at[here], out_ref.at[here, pl.ds((SLOTS - 1) * width, width)], sems.at[part]))
         stores[-1].start()
@@ -614,6 +626,27 @@
     return value, got
 
 
+def both_summed(one, two, axis, beside):
+    count = lax.axis_size(axis)
+    one, two = lax.optimization_barrier((one, two))
+    values, got = [one, two], [jnp.zeros_like(one), jnp.zeros_like(two)]
+    if count & (count - 1):
+        values, count = [lax.psum(value, axis) for value in values], 1
+    d = [1 << bit for bit in range(count.bit_length() - 1)]
+    for place, distances in enumerate(zip(*(d[:1] + d[:0:-1], d[::-1]))):
+        if place:
+            values = [value + came for value, came in zip(values, got)]
+        got = [
+            lax.ppermute(value, axis, [(source, source ^ distance) for source in range(count)])
+            for value, distance in zip(values, distances)
+        ]
+        if beside:
+            values[0] = beside.pop(0)(values[0])
+    for work in beside:
+        values[0] = work(values[0])
+    return values[0], got[0], values[1], got[1]
+
+
 def body(tracks, pixel_order, pairing):
     frames_dev, _, pixel_total = tracks.shape
     row_devices = lax.axis_size("rows")
@@ -652,11 +685,11 @@
     turns, sent = two_rotations(*summed(sums, "rows", [gram_work, order_first, order_rest]))
     came_turn = from_behind(sent, "cols", 1)
     behind_sent = behind_block(chosen, kept["matrix"], turns)
-    behind = from_behind(behind_sent, "cols", -1)
     own, met, cross, pair = meet(chosen, kept["gram"], kept["split"], came[0], turns, behind_sent)
+    behind = from_behind(lax.optimization_barrier((behind_sent, came_turn, met))[0], "cols", -1)
     sums = came_sums(met, came[1], cross, pair, came_turn, own)
 
-    second_turns, sent = two_rotations(*summed(sums, "rows", [turn_work, moved_work]))
+    second_turns, sent = two_rotations(*both_summed(sums, own, "rows", [turn_work, moved_work]))
     behind_turn = from_behind(sent, "cols", -1)
     out = most_slots(chosen, kept["turned"], kept["moved"], second_turns)
     return last_slot(kept["turned"], behind, behind_turn, out)

time: 165 us -> 163 us (0.988)
  waiting for transfers between devices: 99.8 us -> 97.5 us
    ppermute x6 -> x3, waiting for transfers between devices: 6.7 us -> 0.65 us  [summed(): lax.ppermute(value, axis, [(source, source ^ distance) for source in rang...]
    ppermute x0 -> x6, starting transfers between devices: none -> 5.04 us  [both_summed(): lax.ppermute(value, axis, [(source, source ^ distance) for source in rang...]
    ppermute x0 -> x6, waiting for transfers between devices: none -> 3.29 us  [both_summed(): lax.ppermute(value, axis, [(source, source ^ distance) for source in rang...]
    ppermute x6 -> x3, starting transfers between devices: 5.21 us -> 2.9 us  [summed(): lax.ppermute(value, axis, [(source, source ^ distance) for source in rang...]
    ppermute x5, starting transfers between devices: 9.55 us -> 7.76 us  [from_behind(): return lax.ppermute(value, axis, pairs)]
  transfers between devices with their start and end apart: 12 -> 15, of which waited for: 5 -> 7; matrix products, arithmetic and copies ran while one was open for 0% -> 0% of each run, Pallas kernels for 20% -> 20%
where the time goes in v3:
time: 163 us
  waiting for transfers between devices  97.5 us (60%)
  Pallas kernels  41.6 us (26%)
  starting transfers between devices  22.9 us (14%)
    all_to_all x1, waiting for transfers between devices, body(): lax.all_to_all(pieces, ('rows', 'cols'), split_axis=0, concat_axis=0, til...  93.1 us
    pallas_call x2, Pallas kernels, ordered(): pl.pallas_call(functools.partial(order_kernel, *span_of), in_specs=[VMEM]...  9.14 us
    ppermute x5, starting transfers between devices, from_behind(): return lax.ppermute(value, axis, pairs)  7.76 us
    all_to_all x1, starting transfers between devices, body(): lax.all_to_all(pieces, ('rows', 'cols'), split_axis=0, concat_axis=0, til...  7.16 us
    pallas_call x2, Pallas kernels, two_rotations(): pl.pallas_call(rotation_kernel if len(terms) == 2 else later_kernel, in_s...  6.33 us
    ppermute x6, starting transfers between devices, both_summed(): lax.ppermute(value, axis, [(source, source ^ distance) for source in rang...  5.04 us
    pallas_call x1, Pallas kernels, spread(): pl.pallas_call(spread_kernel, in_specs=[ANY], out_specs=HBM, out_shape=ja...  3.49 us
    pallas_call x1, Pallas kernels, couplings(): pl.pallas_call(coupling_kernel, in_specs=[SMEM, ANY], out_specs=[VMEM] *...  3.37 us
  transfers between devices with their start and end apart: 15, of which 7 were waited for; matrix products, arithmetic and copies ran while one was open for 0% of the time, Pallas kernels for 20%

profile of v3, /device:TPU:1, one launch (start us, length us, event | category | flops | bytes accessed | tf_op | source)
XLA Modules:
  0.0 162.7 jit_solution(7234022082651740396)
XLA Ops:
  0.0 0.0 copy-start
  0.0 3.5 %spread.1 = f32[8,4,16,2048]{3,2,1,0:T(8,128)} custom-call(f32[32,2,16384]{2,1,0:T(2,128)} %tracks_ref.1), custom_call_target="tpu_custom_call" | custom-call | bytes 8388608 | tf_op jit(solution)/shard_map/spread/pallas_call | solution.py:114
  3.5 0.0 copy-start.1
  3.5 7.2 %all-to-all-start = ((f32[32,16,2048]{2,1,0:T(8,128)}), f32[32,16,2048]{2,1,0:T(8,128)}, u32[]{:S(2)}, u32[]{:S(2)}) async-start(f32[32,16,2048]{2,1,0:T(8,128)} %bitcast.4), calls=%async_computation | async-start | bytes 8388608 | tf_op jit(solution)/shard_map/all_to_all | solution.py:655
  10.7 0.0 copy-done
  10.7 0.2 dynamic-slice_reduce_fusion.chosen_ref
  10.9 0.0 copy-done.1
  10.9 93.1 %all-to-all-done = f32[32,16,2048]{2,1,0:T(8,128)} async-done(((f32[32,16,2048]{2,1,0:T(8,128)}), f32[32,16,2048]{2,1,0:T(8,128)}, u32[]{:S(2)}, u32[]{:S(2)}) %all-to-all-start) | async-done | bytes 4194336 | tf_op jit(solution)/shard_map/all_to_all | solution.py:655
  104.0 3.4 %couplings.1 = (f32[264,128]{1,0:T(8,128)S(1)}, f32[256,1024]{1,0:T(8,128)S(1)}, f32[256,1024]{1,0:T(8,128)S(1)}, f32[16,512,128]{2,1,0:T(8,128)S(1)}) custom-call(s32[2]{0:T(128)S(1)} %dynamic-slice_reduce_fusion.chosen_ref, f32[512,2048]{1,0:T(8,128)} %bitcast.2.held_ref), custom_call_target="tpu_custom_call" | custom-call | flops 536870912 | bytes 6291456 | tf_op jit(solution)/shard_map/couplings/pallas_call | solution.py:169
  107.4 1.0 collective-permute-start
  108.4 2.5 %collective-permute-start.3 = (f32[256,1024]{1,0:T(8,128)S(1)}, f32[256,1024]{1,0:T(8,128)S(1)}, u32[]{:S(2)}, u32[]{:S(2)}) collective-permute-start(f32[256,1024]{1,0:T(8,128)S(1)} %get-tuple-element.45), channel_id=1, source_target_pairs={{0,1},{1,2},{2,3},{3,0},{4,5},{5,6},{6,7},{7,4},{8,9},{9,10},{10,1... | collective-permute-start | bytes 3145736 | tf_op jit(solution)/shard_map/ppermute | solution.py:608
  110.9 0.0 collective-permute-start.4
  110.9 2.6 %gram.1 = (f32[264,128]{1,0:T(8,128)S(1)}, f32[512,512]{1,0:T(8,128)S(1)}, bf16[1024,2048]{1,0:T(8,128)(2,1)S(1)}) custom-call(f32[264,128]{1,0:T(8,128)S(1)} %get-tuple-element.33.value_ref, f32[16,512,128]{2,1,0:T(8,128)S(1)} %get-tuple-element.34.came_ref), custom_call_target="tpu_custom_call" | custom-call | flops 2147483648 | bytes 8388608 | tf_op jit(solution)/shard_map/gram/pallas_call | solution.py:211
  113.5 0.0 collective-permute-done
  113.6 0.1 collective-permute-start.1
  113.6 1.7 %picks.1 = (f32[264,128]{1,0:T(8,128)S(1)}, bf16[2048,2048]{1,0:T(8,128)(2,1)S(1)}) custom-call(s32[1,2048]{1,0:T(1,128)S(1)} %bitcast.3, f32[264,128]{1,0:T(8,128)S(1)} %add.23.value_ref), custom_call_target="tpu_custom_call" | custom-call | flops 4194304 | bytes 8388608 | tf_op jit(solution)/shard_map/picks/pallas_call | solution.py:421
  115.3 3.4 %row_order.2 = (f32[264,128]{1,0:T(8,128)S(1)}, bf16[2,4,2048,128]{3,2,1,0:T(8,128)(2,1)S(1)}) custom-call(bf16[2048,2048]{1,0:T(8,128)(2,1)S(1)} %get-tuple-element.36.picks_ref, bf16[1024,2048]{1,0:T(8,128)(2,1)S(1)} %get-tuple-element.37.split_ref, f32[264,128]{1,0:T(8,128)S(1)} %get-tuple-element.38.value_ref), custom_call_target="tpu_custom_call" | custom-call | flops 3221225472 | bytes 8388608 | tf_op jit(solution)/shard_map/row_order/pallas_call | solution.py:445
  118.8 0.0 collective-permute-done.1
  118.8 1.8 %collective-permute-start.2 = (f32[264,128]{1,0:T(8,128)S(1)}, f32[264,128]{1,0:T(8,128)S(1)}, u32[]{:S(2)}, u32[]{:S(2)}) collective-permute-start(f32[264,128]{1,0:T(8,128)S(1)} %add.24.value_ref), channel_id=1, source_target_pairs={{0,16},{4,20},{8,24},{12,28},{16,0},{20,4},{24,8},{28,12},{1,17},{... | collective-permute-start | bytes 405512 | tf_op jit(solution)/shard_map/ppermute | solution.py:620
  120.6 5.7 %row_order.3 = (f32[264,128]{1,0:T(8,128)S(1)}, bf16[2,4,2048,128]{3,2,1,0:T(8,128)(2,1)S(1)}) custom-call(bf16[2048,2048]{1,0:T(8,128)(2,1)S(1)} %get-tuple-element.36.picks_ref, bf16[1024,2048]{1,0:T(8,128)(2,1)S(1)} %get-tuple-element.37.split_ref, f32[264,128]{1,0:T(8,128)S(1)} %add.24.value_ref, ...), custom_call_target="tpu_custom_call", output_to_operand_aliasing={{1}: (3, {})} | custom-call | flops 5368709120 | bytes 8388608 | tf_op jit(solution)/shard_map/row_order/pallas_call | solution.py:445
  126.3 0.6 collective-permute-done.2.two_ref
  127.0 3.3 %rotations.2 = (f32[2,256,256]{2,1,0:T(8,128)S(1)}, f32[256,128]{1,0:T(8,128)S(1)}) custom-call(f32[264,128]{1,0:T(8,128)S(1)} %get-tuple-element.42.one_ref, f32[264,128]{1,0:T(8,128)S(1)} %collective-permute-done.2.two_ref), custom_call_target="tpu_custom_call" | custom-call | flops 2516582400 | bytes 262144 | tf_op jit(solution)/shard_map/rotations/pallas_call | solution.py:310
  130.3 1.7 %collective-permute-start.5 = (f32[256,128]{1,0:T(8,128)S(1)}, f32[256,128]{1,0:T(8,128)S(1)}, u32[]{:S(2)}, u32[]{:S(2)}) collective-permute-start(f32[256,128]{1,0:T(8,128)S(1)} %get-tuple-element.50), channel_id=1, source_target_pairs={{0,1},{1,2},{2,3},{3,0},{4,5},{5,6},{6,7},{7,4},{8,9},{9,10},{10,1... | collective-permute-start | bytes 393224 | tf_op jit(solution)/shard_map/ppermute | solution.py:608
  131.9 1.2 behind_block.1._
  133.2 0.0 collective-permute-done.3.came_ref.one_ref
  133.2 2.4 %meet.1 = (f32[136,128]{1,0:T(8,128)S(1)}, bf16[2,128,2048]{2,1,0:T(8,128)(2,1)S(1)}, f32[128,256]{1,0:T(8,128)S(1)}, f32[256,256]{1,0:T(8,128)S(1)}) custom-call(s32[2]{0:T(128)S(1)} %dynamic-slice_reduce_fusion.chosen_ref, f32[512,512]{1,0:T(8,128)S(1)} %get-tuple-element.44.gram_ref, bf16[1024,2048]{1,0:T(8,128)(2,1)S(1)} %get-tuple-element.37.split_ref, ...), custom_call_target="tpu_custom_call" | custom-call | flops 1073741824 | bytes 3932160 | tf_op jit(solution)/shard_map/meet/pallas_call | solution.py:371
  135.6 0.0 collective-permute-done.5.turn_ref
  135.6 0.8 collective-permute-start.6
  136.4 0.0 collective-permute-done.4.came_ref.two_ref
  136.4 1.2 came_sums.1.value_ref
  137.7 0.6 collective-permute-start.7
  138.2 0.0 collective-permute-start.10
  138.2 2.5 %first_turn.1 = (f32[136,128]{1,0:T(8,128)S(1)}, bf16[2,4,2048,128]{3,2,1,0:T(8,128)(2,1)S(1)}) custom-call(s32[2]{0:T(128)S(1)} %dynamic-slice_reduce_fusion.chosen_ref, bf16[2,4,2048,128]{3,2,1,0:T(8,128)(2,1)S(1)} %get-tuple-element.41.matrix_ref, f32[2,256,256]{2,1,0:T(8,128)S(1)} %get-tuple-element.43.rotation_ref, f32[136,128]{1,0:T(8,128)S(1)} %came_sums.1.value_ref), custom_call_target="tpu_custom_call" | custom-call | flops 805306368 | bytes 8388608 | tf_op jit(solution)/shard_map/first_turn/pallas_call | solution.py:499
  140.8 0.1 collective-permute-done.7
  140.9 2.3 %collective-permute-start.8 = (f32[136,128]{1,0:T(8,128)S(1)}, f32[136,128]{1,0:T(8,128)S(1)}, u32[]{:S(2)}, u32[]{:S(2)}) collective-permute-start(f32[136,128]{1,0:T(8,128)S(1)} %add.25.value_ref), channel_id=1, source_target_pairs={{0,16},{4,20},{8,24},{12,28},{16,0},{20,4},{24,8},{28,12},{1,17},{... | collective-permute-start | bytes 208904 | tf_op jit(solution)/shard_map/ppermute | solution.py:640
  143.2 0.5 collective-permute-done.10
  143.7 0.1 collective-permute-start.11
  143.8 3.2 %moved_block.1 = (f32[136,128]{1,0:T(8,128)S(1)}, bf16[2,2048,128]{2,1,0:T(8,128)(2,1)S(1)}) custom-call(bf16[2048,2048]{1,0:T(8,128)(2,1)S(1)} %get-tuple-element.36.picks_ref, f32[256,1024]{1,0:T(8,128)S(1)} %collective-permute-done.3.came_ref.one_ref, f32[256,1024]{1,0:T(8,128)S(1)} %collective-permute-done.4.came_ref.two_ref, ...), custom_call_target="tpu_custom_call" | custom-call | flops 2147483648 | bytes 8388608 | tf_op jit(solution)/shard_map/moved_block/pallas_call | solution.py:521
  147.0 0.0 collective-permute-done.8
  147.0 1.5 collective-permute-start.9
  148.6 0.0 collective-permute-done.11
  148.6 0.5 collective-permute-start.12
  149.1 1.2 collective-permute-done.9.one_got_ref
  150.3 1.5 collective-permute-done.12.two_got_ref
  151.8 3.1 %rotations.3 = (f32[2,256,256]{2,1,0:T(8,128)S(1)}, f32[256,128]{1,0:T(8,128)S(1)}) custom-call(f32[136,128]{1,0:T(8,128)S(1)} %add.26.one_ref, f32[136,128]{1,0:T(8,128)S(1)} %collective-permute-done.9.one_got_ref, f32[136,128]{1,0:T(8,128)S(1)} %add.28.two_ref, f32[136,128]{1,0:T(8,128)S(1)} %collective-permute-done.12.two_got_ref), custom_call_target="tpu_custom_call" | custom-call | flops 2516582400 | bytes 262144 | tf_op jit(solution)/shard_map/rotations/pallas_call | solution.py:310
  154.9 2.8 %collective-permute-start.13 = (f32[256,128]{1,0:T(8,128)S(1)}, f32[256,128]{1,0:T(8,128)S(1)}, u32[]{:S(2)}, u32[]{:S(2)}) collective-permute-start(f32[256,128]{1,0:T(8,128)S(1)} %get-tuple-element.58), channel_id=1, source_target_pairs={{0,3},{1,0},{2,1},{3,2},{4,7},{5,4},{6,5},{7,6},{8,11},{9,8},{10,9... | collective-permute-start | bytes 393224 | tf_op jit(solution)/shard_map/ppermute | solution.py:608
  157.6 3.0 %second_turn.1._ = f32[2048,512]{1,0:T(8,128)} custom-call(s32[2]{0:T(128)S(1)} %dynamic-slice_reduce_fusion.chosen_ref, bf16[2,4,2048,128]{3,2,1,0:T(8,128)(2,1)S(1)} %get-tuple-element.53.turned_ref, bf16[2,2048,128]{2,1,0:T(8,128)(2,1)S(1)} %get-tuple-element.59.moved_ref, f32[2,256,256]{2,1,0:T(8,128)S(1)} %get-tuple-element.60.rotation_ref), custom_call_target="tpu_custom_call" | custom-call | flops 603979776 | bytes 8388608 | tf_op jit(solution)/shard_map/second_turn/pallas_call | solution.py:561
  160.6 0.5 collective-permute-done.13.turn_ref
  161.1 0.0 collective-permute-done.6.behind_ref
  161.1 1.4 last_slot.1
  (7 shorter events, 0.1 us)
Async XLA Ops:
  0.0 10.7 %copy-start = (s32[2,4]{1,0:T(2,128)S(1)}, s32[2,4]{1,0:T(2,128)}, u32[]{:S(2)}) copy-start(s32[2,4]{1,0:T(2,128)} %param.5) | copy-start | bytes 100
  3.5 7.4 %copy-start.1 = (s32[2048]{0:T(1024)S(1)}, s32[2048]{0:T(1024)}, u32[]{:S(2)}) copy-start(s32[2048]{0:T(1024)} %param.4) | copy-start | bytes 24580
  3.5 100.5 %all-to-all-start = ((f32[32,16,2048]{2,1,0:T(8,128)}), f32[32,16,2048]{2,1,0:T(8,128)}, u32[]{:S(2)}, u32[]{:S(2)}) async-start(f32[32,16,2048]{2,1,0:T(8,128)} %bitcast.4), calls=%async_computation | async-start | bytes 8388608 | tf_op jit(solution)/shard_map/all_to_all | solution.py:655
  107.4 6.1 %collective-permute-start = (f32[264,128]{1,0:T(8,128)S(1)}, f32[264,128]{1,0:T(8,128)S(1)}, u32[]{:S(2)}, u32[]{:S(2)}) collective-permute-start(f32[264,128]{1,0:T(8,128)S(1)} %get-tuple-element.33.value_ref), channel_id=1, source_target_pairs={{0,4},{4,0},{8,12},{12,8},{16,20},{20,16},{24,28},{28,24},{1,5},{5... | collective-permute-start | bytes 405512 | tf_op jit(solution)/shard_map/ppermute | solution.py:620
  108.4 24.8 %collective-permute-start.3 = (f32[256,1024]{1,0:T(8,128)S(1)}, f32[256,1024]{1,0:T(8,128)S(1)}, u32[]{:S(2)}, u32[]{:S(2)}) collective-permute-start(f32[256,1024]{1,0:T(8,128)S(1)} %get-tuple-element.45), channel_id=1, source_target_pairs={{0,1},{1,2},{2,3},{3,0},{4,5},{5,6},{6,7},{7,4},{8,9},{9,10},{10,1... | collective-permute-start | bytes 3145736 | tf_op jit(solution)/shard_map/ppermute | solution.py:608
  110.9 25.5 %collective-permute-start.4 = (f32[256,1024]{1,0:T(8,128)S(1)}, f32[256,1024]{1,0:T(8,128)S(1)}, u32[]{:S(2)}, u32[]{:S(2)}) collective-permute-start(f32[256,1024]{1,0:T(8,128)S(1)} %get-tuple-element.47), channel_id=1, source_target_pairs={{0,1},{1,2},{2,3},{3,0},{4,5},{5,6},{6,7},{7,4},{8,9},{9,10},{10,1... | collective-permute-start | bytes 3145736 | tf_op jit(solution)/shard_map/ppermute | solution.py:608
  113.6 5.2 %collective-permute-start.1 = (f32[264,128]{1,0:T(8,128)S(1)}, f32[264,128]{1,0:T(8,128)S(1)}, u32[]{:S(2)}, u32[]{:S(2)}) collective-permute-start(f32[264,128]{1,0:T(8,128)S(1)} %add.23.value_ref), channel_id=1, source_target_pairs={{0,8},{4,12},{8,0},{12,4},{16,24},{20,28},{24,16},{28,20},{1,9},{5... | collective-permute-start | bytes 405512 | tf_op jit(solution)/shard_map/ppermute | solution.py:620
  118.8 8.2 %collective-permute-start.2 = (f32[264,128]{1,0:T(8,128)S(1)}, f32[264,128]{1,0:T(8,128)S(1)}, u32[]{:S(2)}, u32[]{:S(2)}) collective-permute-start(f32[264,128]{1,0:T(8,128)S(1)} %add.24.value_ref), channel_id=1, source_target_pairs={{0,16},{4,20},{8,24},{12,28},{16,0},{20,4},{24,8},{28,12},{1,17},{... | collective-permute-start | bytes 405512 | tf_op jit(solution)/shard_map/ppermute | solution.py:620
  130.3 5.3 %collective-permute-start.5 = (f32[256,128]{1,0:T(8,128)S(1)}, f32[256,128]{1,0:T(8,128)S(1)}, u32[]{:S(2)}, u32[]{:S(2)}) collective-permute-start(f32[256,128]{1,0:T(8,128)S(1)} %get-tuple-element.50), channel_id=1, source_target_pairs={{0,1},{1,2},{2,3},{3,0},{4,5},{5,6},{6,7},{7,4},{8,9},{9,10},{10,1... | collective-permute-start | bytes 393224 | tf_op jit(solution)/shard_map/ppermute | solution.py:608
  135.6 25.4 %collective-permute-start.6 = (f32[2048,128]{1,0:T(8,128)S(1)}, f32[2048,128]{1,0:T(8,128)S(1)}, u32[]{:S(2)}, u32[]{:S(2)}) collective-permute-start(f32[2048,128]{1,0:T(8,128)S(1)} %behind_block.1._), channel_id=1, source_target_pairs={{0,3},{1,0},{2,1},{3,2},{4,7},{5,4},{6,5},{7,6},{8,11},{9,8},{10,9... | collective-permute-start | bytes 3145736 | tf_op jit(solution)/shard_map/ppermute | solution.py:608
  137.7 3.2 %collective-permute-start.7 = (f32[136,128]{1,0:T(8,128)S(1)}, f32[136,128]{1,0:T(8,128)S(1)}, u32[]{:S(2)}, u32[]{:S(2)}) collective-permute-start(f32[136,128]{1,0:T(8,128)S(1)} %came_sums.1.value_ref), channel_id=1, source_target_pairs={{0,4},{4,0},{8,12},{12,8},{16,20},{20,16},{24,28},{28,24},{1,5},{5... | collective-permute-start | bytes 208904 | tf_op jit(solution)/shard_map/ppermute | solution.py:640
  138.2 5.5 %collective-permute-start.10 = (f32[136,128]{1,0:T(8,128)S(1)}, f32[136,128]{1,0:T(8,128)S(1)}, u32[]{:S(2)}, u32[]{:S(2)}) collective-permute-start(f32[136,128]{1,0:T(8,128)S(1)} %get-tuple-element.57.own_ref), channel_id=1, source_target_pairs={{0,16},{4,20},{8,24},{12,28},{16,0},{20,4},{24,8},{28,12},{1,17},{... | collective-permute-start | bytes 208904 | tf_op jit(solution)/shard_map/ppermute | solution.py:640
  140.9 6.1 %collective-permute-start.8 = (f32[136,128]{1,0:T(8,128)S(1)}, f32[136,128]{1,0:T(8,128)S(1)}, u32[]{:S(2)}, u32[]{:S(2)}) collective-permute-start(f32[136,128]{1,0:T(8,128)S(1)} %add.25.value_ref), channel_id=1, source_target_pairs={{0,16},{4,20},{8,24},{12,28},{16,0},{20,4},{24,8},{28,12},{1,17},{... | collective-permute-start | bytes 208904 | tf_op jit(solution)/shard_map/ppermute | solution.py:640
  143.7 4.8 %collective-permute-start.11 = (f32[136,128]{1,0:T(8,128)S(1)}, f32[136,128]{1,0:T(8,128)S(1)}, u32[]{:S(2)}, u32[]{:S(2)}) collective-permute-start(f32[136,128]{1,0:T(8,128)S(1)} %add.27), channel_id=1, source_target_pairs={{0,8},{4,12},{8,0},{12,4},{16,24},{20,28},{24,16},{28,20},{1,9},{5... | collective-permute-start | bytes 208904 | tf_op jit(solution)/shard_map/ppermute | solution.py:640
  147.0 3.2 %collective-permute-start.9 = (f32[136,128]{1,0:T(8,128)S(1)}, f32[136,128]{1,0:T(8,128)S(1)}, u32[]{:S(2)}, u32[]{:S(2)}) collective-permute-start(f32[136,128]{1,0:T(8,128)S(1)} %add.26.one_ref), channel_id=1, source_target_pairs={{0,8},{4,12},{8,0},{12,4},{16,24},{20,28},{24,16},{28,20},{1,9},{5... | collective-permute-start | bytes 208904 | tf_op jit(solution)/shard_map/ppermute | solution.py:640
  148.6 3.2 %collective-permute-start.12 = (f32[136,128]{1,0:T(8,128)S(1)}, f32[136,128]{1,0:T(8,128)S(1)}, u32[]{:S(2)}, u32[]{:S(2)}) collective-permute-start(f32[136,128]{1,0:T(8,128)S(1)} %add.28.two_ref), channel_id=1, source_target_pairs={{0,4},{4,0},{8,12},{12,8},{16,20},{20,16},{24,28},{28,24},{1,5},{5... | collective-permute-start | bytes 208904 | tf_op jit(solution)/shard_map/ppermute | solution.py:640
  154.9 6.2 %collective-permute-start.13 = (f32[256,128]{1,0:T(8,128)S(1)}, f32[256,128]{1,0:T(8,128)S(1)}, u32[]{:S(2)}, u32[]{:S(2)}) collective-permute-start(f32[256,128]{1,0:T(8,128)S(1)} %get-tuple-element.58), channel_id=1, source_target_pairs={{0,3},{1,0},{2,1},{3,2},{4,7},{5,4},{6,5},{7,6},{8,11},{9,8},{10,9... | collective-permute-start | bytes 393224 | tf_op jit(solution)/shard_map/ppermute | solution.py:608

commit v4 on v3

--- a/solution.py
+++ b/solution.py
@@ -689,7 +689,7 @@
     behind = from_behind(lax.optimization_barrier((behind_sent, came_turn, met))[0], "cols", -1)
     sums = came_sums(met, came[1], cross, pair, came_turn, own)
 
-    second_turns, sent = two_rotations(*both_summed(sums, own, "rows", [turn_work, moved_work]))
+    second_turns, sent = two_rotations(*both_summed(sums, own, "rows", [moved_work, turn_work]))
     behind_turn = from_behind(sent, "cols", -1)
     out = most_slots(chosen, kept["turned"], kept["moved"], second_turns)
     return last_slot(kept["turned"], behind, behind_turn, out)

time: 163 us -> 163 us (level)
  transfers between devices with their start and end apart: 15 -> 15, of which waited for: 7 -> 5; matrix products, arithmetic and copies ran while one was open for 0% -> 0% of each run, Pallas kernels for 20% -> 20%
where the time goes in v4:
time: 163 us
  waiting for transfers between devices  96.8 us (59%)
  Pallas kernels  41.6 us (26%)
  starting transfers between devices  24 us (15%)
    all_to_all x1, waiting for transfers between devices, body(): lax.all_to_all(pieces, ('rows', 'cols'), split_axis=0, concat_axis=0, til...  93.1 us
    pallas_call x2, Pallas kernels, ordered(): pl.pallas_call(functools.partial(order_kernel, *span_of), in_specs=[VMEM]...  9.14 us
    ppermute x5, starting transfers between devices, from_behind(): return lax.ppermute(value, axis, pairs)  8.31 us
    all_to_all x1, starting transfers between devices, body(): lax.all_to_all(pieces, ('rows', 'cols'), split_axis=0, concat_axis=0, til...  7.16 us
    pallas_call x2, Pallas kernels, two_rotations(): pl.pallas_call(rotation_kernel if len(terms) == 2 else later_kernel, in_s...  6.31 us
    ppermute x6, starting transfers between devices, both_summed(): lax.ppermute(value, axis, [(source, source ^ distance) for source in rang...  5.6 us
    pallas_call x1, Pallas kernels, spread(): pl.pallas_call(spread_kernel, in_specs=[ANY], out_specs=HBM, out_shape=ja...  3.49 us
    pallas_call x1, Pallas kernels, couplings(): pl.pallas_call(coupling_kernel, in_specs=[SMEM, ANY], out_specs=[VMEM] *...  3.37 us
  transfers between devices with their start and end apart: 15, of which 5 were waited for; matrix products, arithmetic and copies ran while one was open for 0% of the time, Pallas kernels for 20%

profile of v4, /device:TPU:1, one launch (start us, length us, event | category | flops | bytes accessed | tf_op | source)
XLA Modules:
  0.0 163.1 jit_solution(12036279870701237972)
XLA Ops:
  0.0 0.0 copy-start
  0.0 3.5 %spread.1 = f32[8,4,16,2048]{3,2,1,0:T(8,128)} custom-call(f32[32,2,16384]{2,1,0:T(2,128)} %tracks_ref.1), custom_call_target="tpu_custom_call" | custom-call | bytes 8388608 | tf_op jit(solution)/shard_map/spread/pallas_call | solution.py:114
  3.5 0.0 copy-start.1
  3.5 7.2 %all-to-all-start = ((f32[32,16,2048]{2,1,0:T(8,128)}), f32[32,16,2048]{2,1,0:T(8,128)}, u32[]{:S(2)}, u32[]{:S(2)}) async-start(f32[32,16,2048]{2,1,0:T(8,128)} %bitcast.4), calls=%async_computation | async-start | bytes 8388608 | tf_op jit(solution)/shard_map/all_to_all | solution.py:655
  10.7 0.0 copy-done
  10.7 0.2 dynamic-slice_reduce_fusion.chosen_ref
  10.9 0.0 copy-done.1
  10.9 93.1 %all-to-all-done = f32[32,16,2048]{2,1,0:T(8,128)} async-done(((f32[32,16,2048]{2,1,0:T(8,128)}), f32[32,16,2048]{2,1,0:T(8,128)}, u32[]{:S(2)}, u32[]{:S(2)}) %all-to-all-start) | async-done | bytes 4194336 | tf_op jit(solution)/shard_map/all_to_all | solution.py:655
  104.0 3.4 %couplings.1 = (f32[264,128]{1,0:T(8,128)S(1)}, f32[256,1024]{1,0:T(8,128)S(1)}, f32[256,1024]{1,0:T(8,128)S(1)}, f32[16,512,128]{2,1,0:T(8,128)S(1)}) custom-call(s32[2]{0:T(128)S(1)} %dynamic-slice_reduce_fusion.chosen_ref, f32[512,2048]{1,0:T(8,128)} %bitcast.2.held_ref), custom_call_target="tpu_custom_call" | custom-call | flops 536870912 | bytes 6291456 | tf_op jit(solution)/shard_map/couplings/pallas_call | solution.py:169
  107.4 1.0 collective-permute-start
  108.4 2.5 %collective-permute-start.3 = (f32[256,1024]{1,0:T(8,128)S(1)}, f32[256,1024]{1,0:T(8,128)S(1)}, u32[]{:S(2)}, u32[]{:S(2)}) collective-permute-start(f32[256,1024]{1,0:T(8,128)S(1)} %get-tuple-element.44), channel_id=1, source_target_pairs={{0,1},{1,2},{2,3},{3,0},{4,5},{5,6},{6,7},{7,4},{8,9},{9,10},{10,1... | collective-permute-start | bytes 3145736 | tf_op jit(solution)/shard_map/ppermute | solution.py:608
  110.9 0.0 collective-permute-start.4
  110.9 2.6 %gram.1 = (f32[264,128]{1,0:T(8,128)S(1)}, f32[512,512]{1,0:T(8,128)S(1)}, bf16[1024,2048]{1,0:T(8,128)(2,1)S(1)}) custom-call(f32[264,128]{1,0:T(8,128)S(1)} %get-tuple-element.33.value_ref, f32[16,512,128]{2,1,0:T(8,128)S(1)} %get-tuple-element.34.came_ref), custom_call_target="tpu_custom_call" | custom-call | flops 2147483648 | bytes 8388608 | tf_op jit(solution)/shard_map/gram/pallas_call | solution.py:211
  113.5 0.0 collective-permute-done
  113.6 0.1 collective-permute-start.1
  113.6 1.7 %picks.1 = (f32[264,128]{1,0:T(8,128)S(1)}, bf16[2048,2048]{1,0:T(8,128)(2,1)S(1)}) custom-call(s32[1,2048]{1,0:T(1,128)S(1)} %bitcast.3, f32[264,128]{1,0:T(8,128)S(1)} %add.23.value_ref), custom_call_target="tpu_custom_call" | custom-call | flops 4194304 | bytes 8388608 | tf_op jit(solution)/shard_map/picks/pallas_call | solution.py:421
  115.3 3.4 %row_order.2 = (f32[264,128]{1,0:T(8,128)S(1)}, bf16[2,4,2048,128]{3,2,1,0:T(8,128)(2,1)S(1)}) custom-call(bf16[2048,2048]{1,0:T(8,128)(2,1)S(1)} %get-tuple-element.36.picks_ref, bf16[1024,2048]{1,0:T(8,128)(2,1)S(1)} %get-tuple-element.37.split_ref, f32[264,128]{1,0:T(8,128)S(1)} %get-tuple-element.38.value_ref), custom_call_target="tpu_custom_call" | custom-call | flops 3221225472 | bytes 8388608 | tf_op jit(solution)/shard_map/row_order/pallas_call | solution.py:445
  118.8 0.0 collective-permute-done.1
  118.8 1.8 %collective-permute-start.2 = (f32[264,128]{1,0:T(8,128)S(1)}, f32[264,128]{1,0:T(8,128)S(1)}, u32[]{:S(2)}, u32[]{:S(2)}) collective-permute-start(f32[264,128]{1,0:T(8,128)S(1)} %add.24.value_ref), channel_id=1, source_target_pairs={{0,16},{4,20},{8,24},{12,28},{16,0},{20,4},{24,8},{28,12},{1,17},{... | collective-permute-start | bytes 405512 | tf_op jit(solution)/shard_map/ppermute | solution.py:620
  120.6 5.7 %row_order.3 = (f32[264,128]{1,0:T(8,128)S(1)}, bf16[2,4,2048,128]{3,2,1,0:T(8,128)(2,1)S(1)}) custom-call(bf16[2048,2048]{1,0:T(8,128)(2,1)S(1)} %get-tuple-element.36.picks_ref, bf16[1024,2048]{1,0:T(8,128)(2,1)S(1)} %get-tuple-element.37.split_ref, f32[264,128]{1,0:T(8,128)S(1)} %add.24.value_ref, ...), custom_call_target="tpu_custom_call", output_to_operand_aliasing={{1}: (3, {})} | custom-call | flops 5368709120 | bytes 8388608 | tf_op jit(solution)/shard_map/row_order/pallas_call | solution.py:445
  126.3 0.6 collective-permute-done.2.two_ref
  127.0 3.3 %rotations.2 = (f32[2,256,256]{2,1,0:T(8,128)S(1)}, f32[256,128]{1,0:T(8,128)S(1)}) custom-call(f32[264,128]{1,0:T(8,128)S(1)} %get-tuple-element.42.one_ref, f32[264,128]{1,0:T(8,128)S(1)} %collective-permute-done.2.two_ref), custom_call_target="tpu_custom_call" | custom-call | flops 2516582400 | bytes 262144 | tf_op jit(solution)/shard_map/rotations/pallas_call | solution.py:310
  130.3 1.7 %collective-permute-start.5 = (f32[256,128]{1,0:T(8,128)S(1)}, f32[256,128]{1,0:T(8,128)S(1)}, u32[]{:S(2)}, u32[]{:S(2)}) collective-permute-start(f32[256,128]{1,0:T(8,128)S(1)} %get-tuple-element.46), channel_id=1, source_target_pairs={{0,1},{1,2},{2,3},{3,0},{4,5},{5,6},{6,7},{7,4},{8,9},{9,10},{10,1... | collective-permute-start | bytes 393224 | tf_op jit(solution)/shard_map/ppermute | solution.py:608
  131.9 1.2 behind_block.1._
  133.2 0.0 collective-permute-done.3.came_ref.one_ref
  133.2 2.4 %meet.1 = (f32[136,128]{1,0:T(8,128)S(1)}, bf16[2,128,2048]{2,1,0:T(8,128)(2,1)S(1)}, f32[128,256]{1,0:T(8,128)S(1)}, f32[256,256]{1,0:T(8,128)S(1)}) custom-call(s32[2]{0:T(128)S(1)} %dynamic-slice_reduce_fusion.chosen_ref, f32[512,512]{1,0:T(8,128)S(1)} %get-tuple-element.47.gram_ref, bf16[1024,2048]{1,0:T(8,128)(2,1)S(1)} %get-tuple-element.37.split_ref, ...), custom_call_target="tpu_custom_call" | custom-call | flops 1073741824 | bytes 3932160 | tf_op jit(solution)/shard_map/meet/pallas_call | solution.py:371
  135.6 0.0 collective-permute-done.5.turn_ref
  135.6 0.8 collective-permute-start.7
  136.4 0.0 collective-permute-done.4.came_ref.two_ref
  136.4 1.2 came_sums.1.value_ref
  137.7 0.6 collective-permute-start.6
  138.2 0.0 collective-permute-start.10
  138.2 3.2 %moved_block.1 = (f32[136,128]{1,0:T(8,128)S(1)}, bf16[2,2048,128]{2,1,0:T(8,128)(2,1)S(1)}) custom-call(bf16[2048,2048]{1,0:T(8,128)(2,1)S(1)} %get-tuple-element.36.picks_ref, f32[256,1024]{1,0:T(8,128)S(1)} %collective-permute-done.3.came_ref.one_ref, f32[256,1024]{1,0:T(8,128)S(1)} %collective-permute-done.4.came_ref.two_ref, ...), custom_call_target="tpu_custom_call" | custom-call | flops 2147483648 | bytes 8388608 | tf_op jit(solution)/shard_map/moved_block/pallas_call | solution.py:521
  141.4 0.0 collective-permute-done.6
  141.5 2.4 %collective-permute-start.8 = (f32[136,128]{1,0:T(8,128)S(1)}, f32[136,128]{1,0:T(8,128)S(1)}, u32[]{:S(2)}, u32[]{:S(2)}) collective-permute-start(f32[136,128]{1,0:T(8,128)S(1)} %add.25.value_ref), channel_id=1, source_target_pairs={{0,16},{4,20},{8,24},{12,28},{16,0},{20,4},{24,8},{28,12},{1,17},{... | collective-permute-start | bytes 208904 | tf_op jit(solution)/shard_map/ppermute | solution.py:640
  143.9 0.0 collective-permute-done.10
  143.9 0.1 collective-permute-start.11
  144.0 2.5 %first_turn.1 = (f32[136,128]{1,0:T(8,128)S(1)}, bf16[2,4,2048,128]{3,2,1,0:T(8,128)(2,1)S(1)}) custom-call(s32[2]{0:T(128)S(1)} %dynamic-slice_reduce_fusion.chosen_ref, bf16[2,4,2048,128]{3,2,1,0:T(8,128)(2,1)S(1)} %get-tuple-element.41.matrix_ref, f32[2,256,256]{2,1,0:T(8,128)S(1)} %get-tuple-element.43.rotation_ref, f32[136,128]{1,0:T(8,128)S(1)} %add.25.value_ref), custom_call_target="tpu_custom_call" | custom-call | flops 805306368 | bytes 8388608 | tf_op jit(solution)/shard_map/first_turn/pallas_call | solution.py:499
  146.5 0.0 collective-permute-done.8
  146.6 1.5 collective-permute-start.9
  148.1 0.0 collective-permute-done.11
  148.1 1.0 collective-permute-start.12
  149.1 0.7 collective-permute-done.9.one_got_ref
  149.8 1.5 collective-permute-done.12.two_got_ref
  151.3 3.0 %rotations.3 = (f32[2,256,256]{2,1,0:T(8,128)S(1)}, f32[256,128]{1,0:T(8,128)S(1)}) custom-call(f32[136,128]{1,0:T(8,128)S(1)} %add.26.one_ref, f32[136,128]{1,0:T(8,128)S(1)} %collective-permute-done.9.one_got_ref, f32[136,128]{1,0:T(8,128)S(1)} %add.28.two_ref, f32[136,128]{1,0:T(8,128)S(1)} %collective-permute-done.12.two_got_ref), custom_call_target="tpu_custom_call" | custom-call | flops 2516582400 | bytes 262144 | tf_op jit(solution)/shard_map/rotations/pallas_call | solution.py:310
  154.4 3.3 %collective-permute-start.13 = (f32[256,128]{1,0:T(8,128)S(1)}, f32[256,128]{1,0:T(8,128)S(1)}, u32[]{:S(2)}, u32[]{:S(2)}) collective-permute-start(f32[256,128]{1,0:T(8,128)S(1)} %get-tuple-element.58), channel_id=1, source_target_pairs={{0,3},{1,0},{2,1},{3,2},{4,7},{5,4},{6,5},{7,6},{8,11},{9,8},{10,9... | collective-permute-start | bytes 393224 | tf_op jit(solution)/shard_map/ppermute | solution.py:608
  157.7 3.0 %second_turn.1._ = f32[2048,512]{1,0:T(8,128)} custom-call(s32[2]{0:T(128)S(1)} %dynamic-slice_reduce_fusion.chosen_ref, bf16[2,4,2048,128]{3,2,1,0:T(8,128)(2,1)S(1)} %get-tuple-element.54.turned_ref, bf16[2,2048,128]{2,1,0:T(8,128)(2,1)S(1)} %get-tuple-element.59.moved_ref, f32[2,256,256]{2,1,0:T(8,128)S(1)} %get-tuple-element.60.rotation_ref), custom_call_target="tpu_custom_call" | custom-call | flops 603979776 | bytes 8388608 | tf_op jit(solution)/shard_map/second_turn/pallas_call | solution.py:561
  160.7 0.8 collective-permute-done.13.turn_ref
  161.5 0.0 collective-permute-done.7.behind_ref
  161.5 1.4 last_slot.1
  (7 shorter events, 0.1 us)
Async XLA Ops:
  0.0 10.7 %copy-start = (s32[2,4]{1,0:T(2,128)S(1)}, s32[2,4]{1,0:T(2,128)}, u32[]{:S(2)}) copy-start(s32[2,4]{1,0:T(2,128)} %param.5) | copy-start | bytes 100
  3.5 7.4 %copy-start.1 = (s32[2048]{0:T(1024)S(1)}, s32[2048]{0:T(1024)}, u32[]{:S(2)}) copy-start(s32[2048]{0:T(1024)} %param.4) | copy-start | bytes 24580
  3.5 100.5 %all-to-all-start = ((f32[32,16,2048]{2,1,0:T(8,128)}), f32[32,16,2048]{2,1,0:T(8,128)}, u32[]{:S(2)}, u32[]{:S(2)}) async-start(f32[32,16,2048]{2,1,0:T(8,128)} %bitcast.4), calls=%async_computation | async-start | bytes 8388608 | tf_op jit(solution)/shard_map/all_to_all | solution.py:655
  107.4 6.1 %collective-permute-start = (f32[264,128]{1,0:T(8,128)S(1)}, f32[264,128]{1,0:T(8,128)S(1)}, u32[]{:S(2)}, u32[]{:S(2)}) collective-permute-start(f32[264,128]{1,0:T(8,128)S(1)} %get-tuple-element.33.value_ref), channel_id=1, source_target_pairs={{0,4},{4,0},{8,12},{12,8},{16,20},{20,16},{24,28},{28,24},{1,5},{5... | collective-permute-start | bytes 405512 | tf_op jit(solution)/shard_map/ppermute | solution.py:620
  108.4 24.8 %collective-permute-start.3 = (f32[256,1024]{1,0:T(8,128)S(1)}, f32[256,1024]{1,0:T(8,128)S(1)}, u32[]{:S(2)}, u32[]{:S(2)}) collective-permute-start(f32[256,1024]{1,0:T(8,128)S(1)} %get-tuple-element.44), channel_id=1, source_target_pairs={{0,1},{1,2},{2,3},{3,0},{4,5},{5,6},{6,7},{7,4},{8,9},{9,10},{10,1... | collective-permute-start | bytes 3145736 | tf_op jit(solution)/shard_map/ppermute | solution.py:608
  110.9 25.5 %collective-permute-start.4 = (f32[256,1024]{1,0:T(8,128)S(1)}, f32[256,1024]{1,0:T(8,128)S(1)}, u32[]{:S(2)}, u32[]{:S(2)}) collective-permute-start(f32[256,1024]{1,0:T(8,128)S(1)} %get-tuple-element.45), channel_id=1, source_target_pairs={{0,1},{1,2},{2,3},{3,0},{4,5},{5,6},{6,7},{7,4},{8,9},{9,10},{10,1... | collective-permute-start | bytes 3145736 | tf_op jit(solution)/shard_map/ppermute | solution.py:608
  113.6 5.2 %collective-permute-start.1 = (f32[264,128]{1,0:T(8,128)S(1)}, f32[264,128]{1,0:T(8,128)S(1)}, u32[]{:S(2)}, u32[]{:S(2)}) collective-permute-start(f32[264,128]{1,0:T(8,128)S(1)} %add.23.value_ref), channel_id=1, source_target_pairs={{0,8},{4,12},{8,0},{12,4},{16,24},{20,28},{24,16},{28,20},{1,9},{5... | collective-permute-start | bytes 405512 | tf_op jit(solution)/shard_map/ppermute | solution.py:620
  118.8 8.2 %collective-permute-start.2 = (f32[264,128]{1,0:T(8,128)S(1)}, f32[264,128]{1,0:T(8,128)S(1)}, u32[]{:S(2)}, u32[]{:S(2)}) collective-permute-start(f32[264,128]{1,0:T(8,128)S(1)} %add.24.value_ref), channel_id=1, source_target_pairs={{0,16},{4,20},{8,24},{12,28},{16,0},{20,4},{24,8},{28,12},{1,17},{... | collective-permute-start | bytes 405512 | tf_op jit(solution)/shard_map/ppermute | solution.py:620
  130.3 5.3 %collective-permute-start.5 = (f32[256,128]{1,0:T(8,128)S(1)}, f32[256,128]{1,0:T(8,128)S(1)}, u32[]{:S(2)}, u32[]{:S(2)}) collective-permute-start(f32[256,128]{1,0:T(8,128)S(1)} %get-tuple-element.46), channel_id=1, source_target_pairs={{0,1},{1,2},{2,3},{3,0},{4,5},{5,6},{6,7},{7,4},{8,9},{9,10},{10,1... | collective-permute-start | bytes 393224 | tf_op jit(solution)/shard_map/ppermute | solution.py:608
  135.6 25.9 %collective-permute-start.7 = (f32[2048,128]{1,0:T(8,128)S(1)}, f32[2048,128]{1,0:T(8,128)S(1)}, u32[]{:S(2)}, u32[]{:S(2)}) collective-permute-start(f32[2048,128]{1,0:T(8,128)S(1)} %behind_block.1._), channel_id=1, source_target_pairs={{0,3},{1,0},{2,1},{3,2},{4,7},{5,4},{6,5},{7,6},{8,11},{9,8},{10,9... | collective-permute-start | bytes 3145736 | tf_op jit(solution)/shard_map/ppermute | solution.py:608
  137.7 3.8 %collective-permute-start.6 = (f32[136,128]{1,0:T(8,128)S(1)}, f32[136,128]{1,0:T(8,128)S(1)}, u32[]{:S(2)}, u32[]{:S(2)}) collective-permute-start(f32[136,128]{1,0:T(8,128)S(1)} %came_sums.1.value_ref), channel_id=1, source_target_pairs={{0,4},{4,0},{8,12},{12,8},{16,20},{20,16},{24,28},{28,24},{1,5},{5... | collective-permute-start | bytes 208904 | tf_op jit(solution)/shard_map/ppermute | solution.py:640
  138.2 5.7 %collective-permute-start.10 = (f32[136,128]{1,0:T(8,128)S(1)}, f32[136,128]{1,0:T(8,128)S(1)}, u32[]{:S(2)}, u32[]{:S(2)}) collective-permute-start(f32[136,128]{1,0:T(8,128)S(1)} %get-tuple-element.57.own_ref), channel_id=1, source_target_pairs={{0,16},{4,20},{8,24},{12,28},{16,0},{20,4},{24,8},{28,12},{1,17},{... | collective-permute-start | bytes 208904 | tf_op jit(solution)/shard_map/ppermute | solution.py:640
  141.5 5.1 %collective-permute-start.8 = (f32[136,128]{1,0:T(8,128)S(1)}, f32[136,128]{1,0:T(8,128)S(1)}, u32[]{:S(2)}, u32[]{:S(2)}) collective-permute-start(f32[136,128]{1,0:T(8,128)S(1)} %add.25.value_ref), channel_id=1, source_target_pairs={{0,16},{4,20},{8,24},{12,28},{16,0},{20,4},{24,8},{28,12},{1,17},{... | collective-permute-start | bytes 208904 | tf_op jit(solution)/shard_map/ppermute | solution.py:640
  143.9 4.2 %collective-permute-start.11 = (f32[136,128]{1,0:T(8,128)S(1)}, f32[136,128]{1,0:T(8,128)S(1)}, u32[]{:S(2)}, u32[]{:S(2)}) collective-permute-start(f32[136,128]{1,0:T(8,128)S(1)} %add.27), channel_id=1, source_target_pairs={{0,8},{4,12},{8,0},{12,4},{16,24},{20,28},{24,16},{28,20},{1,9},{5... | collective-permute-start | bytes 208904 | tf_op jit(solution)/shard_map/ppermute | solution.py:640
  146.6 3.2 %collective-permute-start.9 = (f32[136,128]{1,0:T(8,128)S(1)}, f32[136,128]{1,0:T(8,128)S(1)}, u32[]{:S(2)}, u32[]{:S(2)}) collective-permute-start(f32[136,128]{1,0:T(8,128)S(1)} %add.26.one_ref), channel_id=1, source_target_pairs={{0,8},{4,12},{8,0},{12,4},{16,24},{20,28},{24,16},{28,20},{1,9},{5... | collective-permute-start | bytes 208904 | tf_op jit(solution)/shard_map/ppermute | solution.py:640
  148.1 3.2 %collective-permute-start.12 = (f32[136,128]{1,0:T(8,128)S(1)}, f32[136,128]{1,0:T(8,128)S(1)}, u32[]{:S(2)}, u32[]{:S(2)}) collective-permute-start(f32[136,128]{1,0:T(8,128)S(1)} %add.28.two_ref), channel_id=1, source_target_pairs={{0,4},{4,0},{8,12},{12,8},{16,20},{20,16},{24,28},{28,24},{1,5},{5... | collective-permute-start | bytes 208904 | tf_op jit(solution)/shard_map/ppermute | solution.py:640
  154.4 7.1 %collective-permute-start.13 = (f32[256,128]{1,0:T(8,128)S(1)}, f32[256,128]{1,0:T(8,128)S(1)}, u32[]{:S(2)}, u32[]{:S(2)}) collective-permute-start(f32[256,128]{1,0:T(8,128)S(1)} %get-tuple-element.58), channel_id=1, source_target_pairs={{0,3},{1,0},{2,1},{3,2},{4,7},{5,4},{6,5},{7,6},{8,11},{9,8},{10,9... | collective-permute-start | bytes 393224 | tf_op jit(solution)/shard_map/ppermute | solution.py:608
